TPU v7x, 128 devices: a whole 4x4x4 slice. The times are simulated.
128 devices in a mesh: ctx: 32 (over z, y, core), head: 4 (over x).
Axes of the slice: x: 4, y: 4, z: 4, core: 2. Of those that a mesh axis runs over, the one named last changes fastest.
Arguments:
- frames: bfloat16 [65536, 1024], P('ctx'), may hold values from -60 to 60, as said below
- len_keys: bfloat16 [256, 65536], P(None, 'ctx'), may hold values from -0.0234375 to 0.0234375
- len_values: bfloat16 [256, 65536], P(None, 'ctx'), may hold values from -0.0234375 to 0.0234375
- w_query: bfloat16 [1024, 1024], P(None, 'head'), may hold values from -0.1875 to 0.1875
- w_key: bfloat16 [1024, 1024], P(None, 'head'), may hold values from -0.1875 to 0.1875
- w_value: bfloat16 [1024, 1024], P(None, 'head'), may hold values from -0.1875 to 0.1875
- w_out: bfloat16 [1024, 1024], P('head'), may hold values from -0.1875 to 0.1875
- cotangent: bfloat16 [65536, 1024], P('ctx', 'head'), may hold values from -6 to 6
Outputs:
- mixed: bfloat16 [65536, 1024], P('ctx', 'head')
- grad_frames: bfloat16 [65536, 1024], P('ctx', 'head')
- grad_wq: float32 [1024, 1024], P(None, 'head')
- grad_wk: float32 [1024, 1024], P(None, 'head')
- grad_wv: float32 [1024, 1024], P(None, 'head')
- grad_wo: float32 [1024, 1024], P('head')
Inputs may be any that keep to these rules, and one draw needn't show every extreme that they name: `frames`: frame features.
All inputs are finite; a program needn't handle non-finite values.
Results may differ from a plain program's by a relative error of at most 0.017.
Values may be sent and summed in bfloat16 or wider, within the bound.
A program may use at most 128 MiB of HBM per device.

v0:
```python
import jax
import jax.numpy as jnp
from jax import lax
from jax.sharding import PartitionSpec as P

DH = 64


def contract_rows(left, right):
    return lax.dot_general(
        left, right, (((0,), (0,)), ((), ())), preferred_element_type=jnp.float32
    )


def contract_cols(left, right):
    return lax.dot_general(
        left, right, (((1,), (1,)), ((), ())), preferred_element_type=jnp.float32
    )


def body(frames, len_keys, len_values, w_query, w_key, w_value, w_out, cotangent):
    scaling = DH ** (-0.5)
    row_count = frames.shape[0]
    col_width = w_query.shape[1]
    head_count = col_width // DH
    proj_len = len_keys.shape[0]
    query = jnp.dot(frames, w_query, preferred_element_type=jnp.float32).astype(jnp.bfloat16)
    keys_full = jnp.dot(frames, w_key, preferred_element_type=jnp.float32).astype(jnp.bfloat16)
    values_full = jnp.dot(frames, w_value, preferred_element_type=jnp.float32).astype(jnp.bfloat16)
    keys_part = jnp.dot(len_keys, keys_full, preferred_element_type=jnp.float32)
    values_part = jnp.dot(len_values, values_full, preferred_element_type=jnp.float32)
    keys_sum, values_sum = lax.psum((keys_part, values_part), "ctx")
    keys_proj = keys_sum.astype(jnp.bfloat16).reshape(proj_len, head_count, DH)
    values_proj = values_sum.astype(jnp.bfloat16).reshape(proj_len, head_count, DH)
    query_heads = query.reshape(row_count, head_count, DH)
    scores = (
        jnp.einsum("shd,khd->hsk", query_heads, keys_proj, preferred_element_type=jnp.float32)
        * scaling
    )
    probab = jax.nn.softmax(scores, axis=-1)
    probab_b = probab.astype(jnp.bfloat16)
    attended_heads = jnp.einsum(
        "hsk,khd->shd", probab_b, values_proj, preferred_element_type=jnp.float32
    )
    attended = attended_heads.reshape(row_count, col_width).astype(jnp.bfloat16)
    out_terms = jnp.dot(attended, w_out, preferred_element_type=jnp.float32)
    mixed = lax.psum_scatter(out_terms, "head", scatter_dimension=1, tiled=True).astype(
        jnp.bfloat16
    )
    cot_full = lax.all_gather(cotangent, "head", axis=1, tiled=True)
    grad_wo_part = contract_rows(attended, cot_full)
    grad_attn = contract_cols(cot_full, w_out).astype(jnp.bfloat16)
    grad_attn_heads = grad_attn.reshape(row_count, head_count, DH)
    grad_prob = jnp.einsum(
        "shd,khd->hsk", grad_attn_heads, values_proj, preferred_element_type=jnp.float32
    )
    grad_vpart = jnp.einsum(
        "hsk,shd->khd", probab_b, grad_attn_heads, preferred_element_type=jnp.float32
    )
    inner = jnp.sum(probab * grad_prob, axis=-1, keepdims=True)
    grad_score = (probab * (grad_prob - inner) * scaling).astype(jnp.bfloat16)
    grad_query = jnp.einsum(
        "hsk,khd->shd", grad_score, keys_proj, preferred_element_type=jnp.float32
    )
    grad_query = grad_query.reshape(row_count, col_width).astype(jnp.bfloat16)
    grad_kpart = jnp.einsum(
        "hsk,shd->khd", grad_score, query_heads, preferred_element_type=jnp.float32
    )
    grad_ksum, grad_vsum = lax.psum(
        (grad_kpart.reshape(proj_len, col_width), grad_vpart.reshape(proj_len, col_width)), "ctx"
    )
    grad_keys = contract_rows(len_keys, grad_ksum.astype(jnp.bfloat16)).astype(jnp.bfloat16)
    grad_values = contract_rows(len_values, grad_vsum.astype(jnp.bfloat16)).astype(jnp.bfloat16)
    frame_terms = (
        contract_cols(grad_query, w_query)
        + contract_cols(grad_keys, w_key)
        + contract_cols(grad_values, w_value)
    )
    grad_frames = lax.psum_scatter(frame_terms, "head", scatter_dimension=1, tiled=True).astype(
        jnp.bfloat16
    )
    wq_part = contract_rows(frames, grad_query)
    wk_part = contract_rows(frames, grad_keys)
    wv_part = contract_rows(frames, grad_values)
    grad_wq, grad_wk, grad_wv, grad_wo = lax.psum((wq_part, wk_part, wv_part, grad_wo_part), "ctx")
    return (mixed, grad_frames, grad_wq, grad_wk, grad_wv, grad_wo)


def solution(mesh):
    placed = (
        P("ctx", None),
        P(None, "ctx"),
        P(None, "ctx"),
        P(None, "head"),
        P(None, "head"),
        P(None, "head"),
        P("head", None),
        P("ctx", "head"),
    )
    return jax.shard_map(
        body,
        mesh=mesh,
        in_specs=placed,
        out_specs=(
            P("ctx", "head"),
            P("ctx", "head"),
            P(None, "head"),
            P(None, "head"),
            P(None, "head"),
            P("head", None),
        ),
        check_vma=False,
    )
```

profile of v0, /device:TPU:1, one launch (start us, length us, event | category | flops | bytes accessed | tf_op | source)
XLA Modules:
  0.0 633.6 jit_solution(14903548977723045708)
XLA Ops:
  7.2 0.0 copy-start
  7.2 0.0 copy-start.8
  7.2 0.0 copy-start.3
  7.2 0.0 all-gather.2.cloned.1.call-start
  7.2 0.7 all-gather.2.cloned.1.call-update
  7.9 0.0 copy-start.6
  8.0 0.0 all-reduce.7.cloned.1.call-start
  8.0 0.4 copy-done
  8.4 4.0 convolution_bitcast_fusion.3
  12.5 4.6 convolution_bitcast_fusion.4
  17.1 129.9 %all-reduce.8 = (bf16[256,256]{0,1:T(8,128)(2,1)S(1)}, bf16[256,256]{0,1:T(8,128)(2,1)S(1)}) all-reduce(f32[256,256]{0,1:T(8,128)} %convolution_bitcast_fusion.4, f32[256,256]{0,1:T(8,128)S(1)} %convolution_bitcast_fusion.3), channel_id=1, replica_groups=mesh['ctx'=32,'head'=4] {'ctx'}, use_global_device_ids=true, to_apply=%region_0.0 | all-reduce | flops 131072 | bytes 786432 | tf_op jit(solution)/shard_map/psum | solution.py:32
  147.0 3.5 convolution_convert_fusion.5
  150.5 0.0 copy-start.12
  150.5 4.9 fusion.30
  155.5 5.3 convolution_convert_fusion
  160.7 3.5 convolution_convert_fusion.3
  164.2 4.5 fusion.32
  168.7 14.3 %fusion.10 = f32[4,64,256]{2,1,0:T(8,128)S(1)} fusion(bf16[2048,4,64]{0,2,1:T(8,128)(2,1)} %bitcast.79, f32[4,2048,256]{1,2,0:T(8,128)} %fusion.32, f32[4,2048,256]{1,2,0:T(8,128)} %get-tuple-element.21, f32[4,2048]{1,0:T(4,128)S(1)} %get-tuple-element.20), kind=kOutput, calls=%fused_computation.11 | convolution fusion | flops 283123968 | bytes 18120704 | tf_op jit(solution)/shard_map/hsk,shd->khd/dot_general | solution.py:66
  183.0 14.8 %fusion.15 = bf16[4,64,2048]{2,1,0:T(8,128)(2,1)} fusion(bf16[256,4,64]{0,2,1:T(8,128)(2,1)S(1)} %bitcast.77, f32[4,2048,256]{1,2,0:T(8,128)} %fusion.32, f32[4,2048,256]{1,2,0:T(8,128)} %get-tuple-element.21, f32[4,2048]{1,0:T(4,128)S(1)} %get-tuple-element.20), kind=kOutput, calls=%fused_computation.14 | convolution fusion | flops 283648256 | bytes 17989632 | tf_op jit(solution)/shard_map/hsk,khd->shd/dot_general | solution.py:62
  197.8 4.8 fusion.18
  202.6 128.4 %all-reduce.9 = (bf16[256,256]{0,1:T(8,128)(2,1)S(1)}, bf16[256,256]{0,1:T(8,128)(2,1)S(1)}) all-reduce(f32[256,256]{0,1:T(8,128)S(1)} %bitcast.72, f32[256,256]{0,1:T(8,128)S(1)} %bitcast.73), channel_id=1, replica_groups=mesh['ctx'=32,'head'=4] {'ctx'}, use_global_device_ids=true, to_apply=%region_6.0 | all-reduce | flops 131072 | bytes 786432 | tf_op jit(solution)/shard_map/psum | solution.py:69
  331.1 0.0 copy-start.10
  331.1 0.4 convolution_convert_fusion.2
  331.5 0.0 copy-start.1
  331.5 1.9 convolution_convert_fusion.1
  333.4 4.4 convolution_bitcast_fusion
  337.8 2.3 convolution_bitcast_fusion.1
  340.1 2.2 convolution_bitcast_fusion.2
  342.4 2.2 fusion.35
  344.6 0.0 all-reduce.7.cloned.1.call-update
  344.6 0.0 reduce-scatter.3.cloned.1.call-start
  344.7 5.9 fusion.31
  350.5 0.0 reduce-scatter.3.cloned.1.call-update
  350.6 0.0 reduce-scatter.5.cloned.1.call-start
  350.6 0.0 copy-start.7
  350.6 2.7 fusion.33
  353.4 1.3 fusion.34
  354.7 4.7 add_add_fusion
  359.4 0.0 reduce-scatter.5.cloned.1.call-update
  359.4 98.8 %all-reduce.7.cloned.1.call-done = (f32[1024,256]{0,1:T(8,128)}, f32[1024,256]{0,1:T(8,128)}, f32[1024,256]{0,1:T(8,128)}, f32[256,1024]{1,0:T(8,128)}) async-done(((f32[1024,256]{0,1:T(8,128)}, f32[1024,256]{0,1:T(8,128)}, f32[1024,256]{0,1:T(8,128)}, f32[256,1024]{1,0:T(8,128)}), (f32[1024,256]{0,1:T(8,128)}, f32[1024,256]{0,1:T(8,128)}, f32[1024,256]{0,1:T(8,128)}, ...) | async-done | bytes 4194320 | tf_op jit(solution)/shard_map/psum | solution.py:85
  458.2 2.6 copy.18
  460.8 2.5 copy.19
  463.4 2.5 copy.20
  465.9 74.9 %reduce-scatter.3.cloned.1.call-done = f32[2048,256]{1,0:T(8,128)} async-done(((f32[2048,1024]{1,0:T(8,128)}), f32[2048,256]{1,0:T(8,128)}) %reduce-scatter.3.cloned.1.call-update) | async-done | bytes 2097168 | tf_op jit(solution)/shard_map/reduce_scatter | solution.py:47
  540.8 2.7 convert_element_type.71
  543.5 79.9 %reduce-scatter.5.cloned.1.call-done = f32[2048,256]{1,0:T(8,128)} async-done(((f32[2048,1024]{1,0:T(8,128)}), f32[2048,256]{1,0:T(8,128)}) %reduce-scatter.5.cloned.1.call-update) | async-done | bytes 2097168 | tf_op jit(solution)/shard_map/reduce_scatter | solution.py:79
  623.4 2.7 convert_element_type.81
  626.1 1.0 copy.37
  (18 shorter events, 0.0 us)
Async XLA Ops:
  7.2 1.2 copy-start
  7.2 5.3 copy-start.8
  7.2 5.3 copy-start.3
  7.2 153.5 %all-gather.2.cloned.1.call-start = ((), (), s32[]{:S(2)}) async-start(), calls=%async_computation.3 | async-start | bytes 5242880 | tf_op jit(solution)/shard_map/all_gather | solution.py:50
  7.9 139.1 %copy-start.6 = (bf16[1024,256]{1,0:T(8,128)(2,1)S(1)}, bf16[1024,256]{1,0:T(8,128)(2,1)}, u32[]{:S(2)}) copy-start(bf16[1024,256]{1,0:T(8,128)(2,1)} %param.11) | copy-start | bytes 1572868
  8.0 450.3 %all-reduce.7.cloned.1.call-start = ((), (), s32[]{:S(2)}) async-start(), calls=%async_computation.5 | async-start | bytes 8388608 | tf_op jit(solution)/shard_map/psum | solution.py:85
  150.5 10.2 %copy-start.12 = (bf16[2048,256]{0,1:T(8,128)(2,1)}, bf16[2048,256]{0,1:T(8,128)(2,1)S(1)}, u32[]{:S(2)}) copy-start(bf16[2048,256]{0,1:T(8,128)(2,1)S(1)} %convolution_convert_fusion.5) | copy-start | bytes 3145732
  155.4 5.3 copy-start.5
  331.1 6.8 %copy-start.10 = (bf16[2048,1024]{1,0:T(8,128)(2,1)S(1)}, bf16[2048,1024]{1,0:T(8,128)(2,1)}, u32[]{:S(2)}) copy-start(bf16[2048,1024]{1,0:T(8,128)(2,1)} %param.8) | copy-start | bytes 12582916
  331.5 8.6 %copy-start.1 = (bf16[4,64,2048]{2,1,0:T(8,128)(2,1)S(1)}, bf16[4,64,2048]{2,1,0:T(8,128)(2,1)}, u32[]{:S(2)}) copy-start(bf16[4,64,2048]{2,1,0:T(8,128)(2,1)} %fusion.15) | copy-start | bytes 3145732
  337.8 4.5 copy-start.2
  337.8 4.5 copy-start.11
  344.6 196.2 %reduce-scatter.3.cloned.1.call-start = ((), (), s32[]{:S(2)}) async-start(), calls=%async_computation.2 | async-start | bytes 10485760 | tf_op jit(solution)/shard_map/reduce_scatter | solution.py:47
  350.6 272.8 %reduce-scatter.5.cloned.1.call-start = ((), (), s32[]{:S(2)}) async-start(), calls=%async_computation.4 | async-start | bytes 10485760 | tf_op jit(solution)/shard_map/reduce_scatter | solution.py:79
  350.6 2.7 copy-start.7
  353.4 1.3 copy-start.9
  458.2 167.8 %copy-start.4 = (f32[256,1024]{1,0:T(8,128)S(1)}, f32[256,1024]{1,0:T(8,128)}, u32[]{:S(2)}) copy-start(f32[256,1024]{1,0:T(8,128)} %get-tuple-element.27) | copy-start | bytes 3145732
Sparse Core Ops, SparseCore 0:
  9.7 54.2 all-gather.1
  344.7 113.4 all-reduce.6
  460.7 80.0 reduce-scatter.2
  543.2 80.2 reduce-scatter.4
where the time goes:
time: 634 us
  blocking collectives  258 us (41%)
  waiting for transfers between devices  254 us (40%)
  matrix products  92.3 us (15%)
  between operations  14 us (2%)
  local copies, waits for them, and re-layouts  9.12 us (1%)
    psum x1, blocking collectives, body(): keys_sum, values_sum = lax.psum((keys_part, values_part), 'ctx')  130 us
    psum x1, blocking collectives, body(): lax.psum((grad_kpart.reshape(proj_len, col_width), grad_vpart.reshape(pro...  128 us
    psum x1, waiting for transfers between devices, body(): lax.psum((wq_part, wk_part, wv_part, grad_wo_part), 'ctx')  98.8 us
    reduce_scatter x1, waiting for transfers between devices, body(): lax.psum_scatter(frame_terms, 'head', scatter_dimension=1, tiled=True)  79.9 us
    reduce_scatter x1, waiting for transfers between devices, body(): lax.psum_scatter(out_terms, 'head', scatter_dimension=1, tiled=True)  74.9 us
    dot_general x1, matrix products, body(): jnp.einsum('hsk,khd->shd', grad_score, keys_proj, preferred_element_type=...  14.8 us
    dot_general x1, matrix products, body(): jnp.einsum('hsk,shd->khd', grad_score, query_heads, preferred_element_typ...  14.3 us
    dot_general x6, matrix products, contract_rows(): lax.dot_general(left, right, (((0,), (0,)), ((), ())), preferred_element_...  13.5 us
  transfers between devices with their start and end apart: 4, of which 3 were waited for; matrix products, arithmetic and copies ran while one was open for 7% of the time, Pallas kernels for 0%

commit v1 on v0

v1 whole, which is shorter than its diff:
```python
import functools

import jax
import jax.numpy as jnp
from jax import lax
from jax.experimental import pallas as pl
from jax.experimental.pallas import tpu as pltpu
from jax.sharding import PartitionSpec as P

DH = 64
MESH = pl.DeviceIdType.MESH
BF = jnp.bfloat16
F32 = jnp.float32


def dot(a, b):
    return jnp.dot(a, b, preferred_element_type=F32)


def dot_nt(a, b):
    return lax.dot_general(a, b, (((1,), (1,)), ((), ())), preferred_element_type=F32)


def flip(a):
    return a.astype(F32).T.astype(BF)


class Sems:
    def __init__(self, ref):
        self.ref, self.used = ref, 0

    def new(self):
        self.used += 1
        return self.ref.at[self.used - 1]


def kernel(
    frames, len_keys, len_values, w_query, w_key, w_value, w_out, cotangent,
    mixed_o, gframes_o, gwq_o, gwk_o, gwv_o, gwo_o,
    fcols, frows, lens, len_t, wqf, wof, wkv, cot,
    fpart, fpair, fsum, frs, fx, kpx, ff, kvp,
    q, ga, prob, att_t, att, gq_t, gq,
    mix_s, mix_r, gf_s, gf_r,
    gkv, gkv_pair, gkv_sum, gkv_rs, gkv_x, gkv_xr, gk16, m_s, m_r, gkm,
    w_s, w_pair, w_sum, w_rs, w_x, w_xr, w_ag, w_f, sem_ref,
):
    sems = Sems(sem_ref)
    me = lax.axis_index("ctx")
    x = lax.axis_index("head")
    core = lax.rem(me, 2)
    chip = lax.div(me, 2)
    other = me + 1 - 2 * core
    rows = frows.shape[0]
    n_x = 4
    n_chip = 16
    width = 256

    def load(src, dst):
        copy = pltpu.make_async_copy(src, dst, sems.new())
        copy.start()
        return copy

    my_cols = pl.ds(pl.multiple_of(x * width, width), width)
    my_rows = pl.ds(pl.multiple_of(x * rows, rows), rows)
    in_f = [load(frames.at[:, my_cols], fcols), load(len_keys, lens.at[0]), load(len_values, lens.at[1])]
    in_q = [load(frames.at[my_rows, :], frows), load(w_query, wqf.at[x])]
    in_c = [load(w_out, wof.at[x]), load(cotangent.at[my_rows, :], cot.at[:, my_cols])]
    in_k = [load(w_key, wkv.at[0]), load(w_value, wkv.at[1])]

    barrier = pltpu.get_barrier_semaphore()
    pl.semaphore_signal(barrier, inc=1, device_id=(other, x), device_id_type=MESH)
    for dx in range(1, n_x):
        pl.semaphore_signal(
            barrier, inc=1, device_id=(me, lax.rem(x + dx, n_x)), device_id_type=MESH
        )

    @pl.loop(1, n_chip)
    def _(d):
        pl.semaphore_signal(
            barrier, inc=1, device_id=(lax.rem(me + 2 * d, 2 * n_chip), x), device_id_type=MESH
        )

    pl.semaphore_wait(barrier, 1 + (n_x - 1) + (n_chip - 1))

    sent = []

    def landed(ref, sem):
        pltpu.make_async_copy(ref, ref, sem).wait()

    def to_other(src, dst):
        s, r = sems.new(), sems.new()
        pltpu.make_async_remote_copy(src, dst, s, r, device_id=(other, x), device_id_type=MESH).start()
        sent.append((src, s))
        return lambda: landed(dst, r)

    def to_x(src, dst, three):
        s, r = sems.new(), sems.new()
        for dx in (2, 1, 3):
            peer = lax.rem(x + dx, n_x)
            pltpu.make_async_remote_copy(
                src(peer), dst(n_x - dx), s, r, device_id=(me, peer), device_id_type=MESH
            ).start()
        sent.append((three, s))
        return lambda: landed(three, r)

    def to_chips(src, dst, fifteen):
        s, r = sems.new(), sems.new()

        @pl.loop(1, n_chip)
        def _(d):
            peer = lax.rem(chip + d, n_chip)
            pltpu.make_async_remote_copy(
                src(peer), dst(n_chip - d), s, r, device_id=(2 * peer + core, x), device_id_type=MESH
            ).start()

        sent.append((fifteen, s))
        return lambda: landed(fifteen, r)

    def piece(i):
        return pl.ds(pl.multiple_of(i * 16, 16), 16)

    hq = pl.ds(pl.multiple_of(core * 512, 512), 512)
    ho = pl.ds(pl.multiple_of(core * 128, 128), 128)
    got_wq = to_x(lambda p: w_query.at[hq, :], lambda o: wqf.at[x, hq, :], wqf.at[0:3, 0:512, :])
    got_cot = to_x(
        lambda p: cotangent.at[pl.ds(pl.multiple_of(p * rows, rows), rows), :],
        lambda o: cot.at[:, my_cols],
        cot.at[:, 0 : 3 * width],
    )
    got_wo = to_x(lambda p: w_out.at[ho, :], lambda o: wof.at[x, ho, :], wof.at[0:3, 0:128, :])

    for copy in in_f:
        copy.wait()

    @pl.loop(0, 2)
    def _(t):
        fpart[t] = dot(lens[t], fcols[...]).astype(BF)

    got_f = to_other(fpart.at[1 - core], fpair)

    @pl.loop(0, 2)
    def _(t):
        @pl.loop(0, 4)
        def _(b):
            at = pl.ds(pl.multiple_of(b * 512, 512), 512)
            len_t[t, at, :] = flip(lens[t, :, at])

    got_f()
    fsum[...] = (fpart[core].astype(F32) + fpair[...].astype(F32)).astype(BF)
    got_frs = to_chips(lambda j: fsum.at[piece(j), :], lambda o: frs.at[o], frs.at[1:n_chip])

    for copy in in_q + in_k:
        copy.wait()
    got_frs()
    total = fsum[piece(chip), :].astype(F32)
    for o in range(1, n_chip):
        total = total + frs[o].astype(F32)
    fx[x] = total.astype(BF)
    got_fx = to_x(lambda p: fx.at[x], lambda o: fx.at[x], fx.at[0:3])
    got_fx()
    total = dot(fx[0], wkv[core, 0:width, :])
    for b in range(1, n_x):
        total = total + dot(fx[b], wkv[core, b * width : (b + 1) * width, :])
    kpx[x] = total.astype(BF)
    got_kpx = to_x(lambda p: kpx.at[x], lambda o: kpx.at[x], kpx.at[0:3])

    def gather(src, full, fifteen):
        copy = load(src, full(core, chip))
        done = to_chips(lambda j: src, lambda o: full(core, chip), fifteen)

        def arrive():
            copy.wait()
            done()

        return arrive

    got_kpx()
    got_kvp = gather(kpx, lambda t, j: kvp.at[t, :, piece(j), :], kvp.at[0, :, 0:240, :])
    got_ff = gather(fx, lambda t, j: ff.at[t, :, piece(j), :], ff.at[0, :, 0:240, :])

    got_wq()
    s, r_wq = sems.new(), sems.new()
    for dx in range(1, n_x):
        b = lax.rem(x + dx, n_x)
        pltpu.make_async_remote_copy(
            wqf.at[b, hq, :], wqf.at[b, hq, :], s, r_wq, device_id=(other, x), device_id_type=MESH
        ).start()
    sent.append((wqf.at[0:3, 0:512, :], s))
    landed(wqf.at[0:3, 0:512, :], r_wq)

    @pl.loop(0, n_x)
    def _(g):
        q[g] = dot(frows[...], wqf[g]).astype(BF)

    got_kvp()
    got_kvo = to_other(kvp.at[core], kvp.at[core])
    got_wo()
    s, r_wo = sems.new(), sems.new()
    for dx in range(1, n_x):
        b = lax.rem(x + dx, n_x)
        pltpu.make_async_remote_copy(
            wof.at[b, ho, :], wof.at[b, ho, :], s, r_wo, device_id=(other, x), device_id_type=MESH
        ).start()
    sent.append((wof.at[0:3, 0:128, :], s))
    landed(wof.at[0:3, 0:128, :], r_wo)
    for copy in in_c:
        copy.wait()
    got_cot()

    @pl.loop(0, n_x)
    def _(g):
        ga[g] = dot_nt(cot[...], wof[g]).astype(BF)

    got_ff()
    got_ffo = to_other(ff.at[core], ff.at[core])
    got_kvo()

    lane = lax.broadcasted_iota(jnp.int32, (width, width), 1) // DH

    def only(h, a):
        return jnp.where(lane == h, a.astype(F32), 0.0).astype(BF)

    @pl.loop(0, n_x)
    def _(g):
        kg = kvp[0, g]
        vg_t = flip(kvp[1, g])
        qg = q[g]
        for h in range(4):
            scores = dot_nt(only(h, kg), qg)
            top = jnp.max(scores, axis=0, keepdims=True)
            e = jnp.exp((scores - top) * (DH ** -0.5))
            p = (e * (1.0 / jnp.sum(e, axis=0, keepdims=True))).astype(BF)
            prob[4 * g + h] = p
            att_t[g, h * DH : (h + 1) * DH, :] = dot(vg_t[h * DH : (h + 1) * DH, :], p).astype(BF)
        att[g] = flip(att_t[g])

    @pl.loop(0, n_x)
    def _(n):
        at = pl.ds(pl.multiple_of(n * width, width), width)
        total = dot(att[0], wof[0, :, at])
        for g in range(1, n_x):
            total = total + dot(att[g], wof[g, :, at])
        mix_s[n] = total.astype(BF)

    got_mix = to_x(
        lambda p: mix_s.at[p], lambda o: mix_r.at[my_rows, :], mix_r.at[0 : 3 * rows, :]
    )
    own_mix = load(mix_s.at[x], mix_r.at[my_rows, :])

    half = w_pair.shape[-1]
    mine = pl.ds(pl.multiple_of(core * half, half), half)
    theirs = pl.ds(pl.multiple_of((1 - core) * half, half), half)

    @pl.loop(0, n_x)
    def _(g):
        w_s[0, g] = dot(att_t[g], cot[...]).astype(BF)

    got_wpair = [to_other(w_s.at[0, :, :, theirs], w_pair.at[0])]

    @pl.loop(0, n_x)
    def _(g):
        vg = kvp[1, g]
        kg_t = flip(kvp[0, g])
        qg = q[g]
        gag = ga[g]
        gk = jnp.zeros((width, width), F32)
        gv = jnp.zeros((width, width), F32)
        for h in range(4):
            pb = prob[4 * g + h]
            p = pb.astype(F32)
            gp = dot_nt(only(h, vg), gag)
            inner = jnp.sum(p * gp, axis=0, keepdims=True)
            gs = (p * (gp - inner) * (DH ** -0.5)).astype(BF)
            gq_t[g, h * DH : (h + 1) * DH, :] = dot(kg_t[h * DH : (h + 1) * DH, :], gs).astype(BF)
            gk = jnp.where(lane == h, dot(gs, qg), gk)
            gv = jnp.where(lane == h, dot(pb, gag), gv)
        gkv[0, g] = gk.astype(BF)
        gkv[1, g] = gv.astype(BF)
        gq[g] = flip(gq_t[g])

    got_gpair = to_other(gkv.at[1 - core], gkv_pair)

    def pair_sum(k):
        got_wpair[k]()

        @pl.loop(0, n_x)
        def _(g):
            w_sum[k, g] = (w_s[k, g, :, mine].astype(F32) + w_pair[k, g].astype(F32)).astype(BF)

        return to_chips(
            lambda j: w_sum.at[k, :, piece(j), :], lambda o: w_rs.at[k, o], w_rs.at[k, 1:n_chip]
        )

    @pl.loop(0, n_x)
    def _(n):
        at = pl.ds(pl.multiple_of(n * width, width), width)
        total = dot_nt(gq[0], wqf[0, at, :])
        for g in range(1, n_x):
            total = total + dot_nt(gq[g], wqf[g, at, :])
        gf_s[n] = total.astype(BF)

    got_gf = to_x(lambda p: gf_s.at[p], lambda o: gf_r.at[my_rows, :], gf_r.at[0 : 3 * rows, :])
    own_gf = load(gf_s.at[x], gf_r.at[my_rows, :])

    got_gpair()

    @pl.loop(0, n_x)
    def _(g):
        gkv_sum[g] = (gkv[core, g].astype(F32) + gkv_pair[g].astype(F32)).astype(BF)

    got_grs = to_chips(lambda j: gkv_sum.at[:, piece(j), :], lambda o: gkv_rs.at[o], gkv_rs.at[1:n_chip])

    @pl.loop(0, n_x)
    def _(g):
        w_s[1, g] = dot(gq_t[g], frows[...]).astype(BF)

    got_wpair.append(to_other(w_s.at[1, :, :, theirs], w_pair.at[1]))
    got_wrs = [pair_sum(0)]

    got_grs()
    total = gkv_sum[:, piece(chip), :].astype(F32)
    for o in range(1, n_chip):
        total = total + gkv_rs[o].astype(F32)
    gkv_x[...] = total.astype(BF)
    got_gx = to_x(lambda p: gkv_x.at[p], lambda o: gkv_xr.at[o], gkv_xr.at[1:n_x])
    got_wrs.append(pair_sum(1))
    got_gx()
    total = gkv_x[x].astype(F32)
    for o in range(1, n_x):
        total = total + gkv_xr[o].astype(F32)
    g16 = total.astype(BF)
    gk16[0] = g16
    for n in range(n_x):
        m_s[n] = dot_nt(g16, wkv[core, n * width : (n + 1) * width, :]).astype(BF)
    got_m = to_x(lambda p: m_s.at[p], lambda o: m_r.at[o], m_r.at[1:n_x])

    def over_x(k):
        got_wrs[k]()
        total = w_sum[k, :, piece(chip), :].astype(F32)
        for o in range(1, n_chip):
            total = total + w_rs[k, o].astype(F32)
        w_x[k] = total.astype(BF)
        return to_x(lambda p: w_x.at[k, p], lambda o: w_xr.at[k, o], w_xr.at[k, 1:n_x])

    got_m()
    total = m_s[x].astype(F32)
    for o in range(1, n_x):
        total = total + m_r[o].astype(F32)
    gk16[1] = total.astype(BF)
    got_gkm = gather(gk16, lambda t, j: gkm.at[t, :, piece(j), :], gkm.at[0, :, 0:240, :])

    got_wx = [over_x(0)]
    got_wx.append(over_x(1))

    def gather_w(k):
        got_wx[k]()
        total = w_x[k, x].astype(F32)
        for o in range(1, n_x):
            total = total + w_xr[k, o].astype(F32)
        w_f[k] = total.astype(BF)
        return gather(w_f.at[k], lambda t, j: w_ag.at[k, t, piece(j), :], w_ag.at[k, 0, 0:240, :])

    got_ffo()
    got_gkm()
    got_gkmo = to_other(gkm.at[core], gkm.at[core])
    got_w = [gather_w(0)]
    got_w.append(gather_w(1))
    outs = []
    own_mix.wait()
    got_mix()
    outs.append(load(mix_r, mixed_o))
    own_gf.wait()
    got_gf()
    got_gkmo()

    @pl.loop(0, n_x)
    def _(b):
        at = pl.ds(pl.multiple_of(b * rows, rows), rows)
        total = gf_r[at, :].astype(F32) + dot(len_t[0, at, :], gkm[0, 1]) + dot(len_t[1, at, :], gkm[1, 1])
        gf_r[at, :] = total.astype(BF)

    outs.append(load(gf_r, gframes_o))
    got_wo2 = []
    for k in range(2):
        got_w[k]()
        got_wo2.append(to_other(w_ag.at[k, core], w_ag.at[k, core]))

    @pl.loop(0, n_x)
    def _(g):
        at = pl.ds(pl.multiple_of(g * width, width), width)
        gwk_o[at, :] = dot(flip(ff[0, g]), gkm[0, 0])
        gwv_o[at, :] = dot(flip(ff[1, g]), gkm[1, 0])

    got_wo2[0]()
    for t in range(2):
        gwo_o[:, t * half : (t + 1) * half] = w_ag[0, t].astype(F32)
    got_wo2[1]()
    for t in range(2):
        gwq_o[t * half : (t + 1) * half, :] = w_ag[1, t].astype(F32).T
    for ref, sem in sent:
        landed(ref, sem)
    for copy in outs:
        copy.wait()


def body(frames, len_keys, len_values, w_query, w_key, w_value, w_out, cotangent):
    span, depth = frames.shape
    rows = span // 4
    bf = lambda *shape: pltpu.VMEM(shape, BF)
    scratch = [
        bf(span, 256), bf(rows, depth), bf(2, 256, span), bf(2, span, 256),
        bf(4, 1024, 256), bf(4, 256, 1024), bf(2, 1024, 256), bf(rows, depth),
        bf(2, 256, 256), bf(256, 256), bf(256, 256), bf(16, 16, 256),
        bf(4, 16, 256), bf(4, 16, 256), bf(2, 4, 256, 256), bf(2, 4, 256, 256),
        bf(4, rows, 256), bf(4, rows, 256), bf(16, 256, rows),
        bf(4, 256, rows), bf(4, rows, 256), bf(4, 256, rows), bf(4, rows, 256),
        bf(4, rows, 256), bf(span, 256), bf(4, rows, 256), bf(span, 256),
        bf(2, 4, 256, 256), bf(4, 256, 256), bf(4, 256, 256), bf(16, 4, 16, 256),
        bf(4, 16, 256), bf(4, 16, 256), bf(2, 16, 256), bf(4, 16, 256), bf(4, 16, 256),
        bf(2, 2, 256, 256),
        bf(2, 4, 256, 1024), bf(2, 4, 256, 512), bf(2, 4, 256, 512), bf(2, 16, 4, 16, 512),
        bf(2, 4, 16, 512), bf(2, 4, 16, 512), bf(2, 2, 256, 512), bf(2, 16, 512),
        pltpu.SemaphoreType.DMA((80,)),
    ]
    any_ = pl.BlockSpec(memory_space=pl.ANY)
    vm = pl.BlockSpec(memory_space=pltpu.VMEM)
    return pl.pallas_call(
        kernel,
        out_shape=(
            jax.ShapeDtypeStruct((span, 256), BF),
            jax.ShapeDtypeStruct((span, 256), BF),
            jax.ShapeDtypeStruct((depth, 256), F32),
            jax.ShapeDtypeStruct((depth, 256), F32),
            jax.ShapeDtypeStruct((depth, 256), F32),
            jax.ShapeDtypeStruct((256, depth), F32),
        ),
        in_specs=[any_] * 8,
        out_specs=(any_, any_, vm, vm, vm, vm),
        scratch_shapes=scratch,
        compiler_params=pltpu.CompilerParams(
            collective_id=0, has_side_effects=True, vmem_limit_bytes=60 * 1024 * 1024
        ),
        cost_estimate=pl.CostEstimate(flops=14_000_000_000, bytes_accessed=24_000_000, transcendentals=2_097_152),
    )(frames, len_keys, len_values, w_query, w_key, w_value, w_out, cotangent)


def solution(mesh):
    placed = (
        P("ctx", None),
        P(None, "ctx"),
        P(None, "ctx"),
        P(None, "head"),
        P(None, "head"),
        P(None, "head"),
        P("head", None),
        P("ctx", "head"),
    )
    return jax.shard_map(
        body,
        mesh=mesh,
        in_specs=placed,
        out_specs=(
            P("ctx", "head"),
            P("ctx", "head"),
            P(None, "head"),
            P(None, "head"),
            P(None, "head"),
            P("head", None),
        ),
        check_vma=False,
    )
```

time: 634 us -> 146 us (0.23)
  blocking collectives: 258 us -> 0 us
  waiting for transfers between devices: 254 us -> 0 us
  Pallas kernels: 0 us -> 136 us
  matrix products: 92.3 us -> 0 us
  between operations: 14 us -> 0.67 us
    psum x2 -> x0, blocking collectives: 258 us -> none  [the longest x1 130 us: body(): keys_sum, values_sum = lax.psum((keys_part, values_part), 'ctx')]
    reduce_scatter x2 -> x0, waiting for transfers between devices: 155 us -> none  [the longest x1 79.9 us: body(): lax.psum_scatter(frame_terms, 'head', scatter_dimension=1, tiled=True)]
    pallas_call x0 -> x1, Pallas kernels: none -> 136 us  [body(): pl.pallas_call(kernel, out_shape=(jax.ShapeDtypeStruct((span, 256), BF),...]
    psum x1 -> x0, waiting for transfers between devices: 98.8 us -> none  [body(): lax.psum((wq_part, wk_part, wv_part, grad_wo_part), 'ctx')]
    dot_general x19 -> x0, matrix products: 87.4 us -> none  [the longest x1 14.8 us: body(): jnp.einsum('hsk,khd->shd', grad_score, keys_proj, preferred_element_type=...]
  transfers between devices with their start and end apart: 4 -> 0, of which waited for: 3 -> 0; matrix products, arithmetic and copies ran while one was open for 7% -> 0% of each run, Pallas kernels for 0% -> 0%
where the time goes in v1:
time: 146 us
  Pallas kernels  136 us (93%)
  local copies, waits for them, and re-layouts  8.66 us (6%)
    pallas_call x1, Pallas kernels, body(): pl.pallas_call(kernel, out_shape=(jax.ShapeDtypeStruct((span, 256), BF),...  136 us
    unnamed x14, local copies, waits for them, and re-layouts  8.66 us

profile of v1, /device:TPU:1, one launch (start us, length us, event | category | flops | bytes accessed | tf_op | source)
XLA Modules:
  0.0 145.6 jit_solution(15349335608100922292)
XLA Ops:
  0.6 136.2 %shard_map.127 = (bf16[2048,256]{1,0:T(8,128)(2,1)}, bf16[2048,256]{1,0:T(8,128)(2,1)}, f32[1024,256]{1,0:T(8,128)}, f32[1024,256]{1,0:T(8,128)}, f32[1024,256]{1,0:T(8,128)}, /*index=5*/f32[256,1024]{1,0:T(8,128)}) custom-call(bf16[2048,1024]{1,0:T(8,128)(2,1)} %frames.1, bf16[256,2048]{1,0:T(8,128)(2,1)} %len_keys.1, bf16[256,2048]{1,0:T(8,128)(2,1)} %len_values.1, ...), custom_call_target="tpu_custom_call" | custom-call | flops 14000000000 | bytes 24000000 | tf_op jit(solution)/shard_map/pallas_call | solution.py:427
  136.9 0.0 copy-start.3
  136.9 0.0 copy-start.2
  136.9 0.0 copy-start.1
  136.9 2.4 %copy.20 = bf16[2048,256]{1,0:T(8,128)(2,1)} copy(bf16[2048,256]{1,0:T(8,128)(2,1)} %get-tuple-element.12) | data formatting | bytes 2097152
  139.3 0.0 copy-start
  139.3 2.4 %copy.21 = bf16[2048,256]{1,0:T(8,128)(2,1)} copy(bf16[2048,256]{1,0:T(8,128)(2,1)} %get-tuple-element.13) | data formatting | bytes 2097152
  141.7 0.0 copy-done.3
  141.7 1.0 copy.22
  142.7 0.0 copy-done.2
  142.7 1.0 copy.23
  143.6 0.0 copy-done.1
  143.6 1.0 copy.24
  144.6 0.0 copy-done
  144.6 1.0 copy.25
Async XLA Ops:
  136.9 4.8 %copy-start.3 = (f32[1024,256]{1,0:T(8,128)S(1)}, f32[1024,256]{1,0:T(8,128)}, u32[]{:S(2)}) copy-start(f32[1024,256]{1,0:T(8,128)} %get-tuple-element.14) | copy-start | bytes 3145732
  136.9 5.8 %copy-start.2 = (f32[1024,256]{1,0:T(8,128)S(1)}, f32[1024,256]{1,0:T(8,128)}, u32[]{:S(2)}) copy-start(f32[1024,256]{1,0:T(8,128)} %get-tuple-element.15) | copy-start | bytes 3145732
  136.9 6.7 %copy-start.1 = (f32[1024,256]{1,0:T(8,128)S(1)}, f32[1024,256]{1,0:T(8,128)}, u32[]{:S(2)}) copy-start(f32[1024,256]{1,0:T(8,128)} %get-tuple-element.16) | copy-start | bytes 3145732
  139.3 5.3 %copy-start = (f32[256,1024]{1,0:T(8,128)S(1)}, f32[256,1024]{1,0:T(8,128)}, u32[]{:S(2)}) copy-start(f32[256,1024]{1,0:T(8,128)} %get-tuple-element.17) | copy-start | bytes 3145732

commit v2 on v0

v2 whole, which is shorter than its diff:
```python
import jax
import jax.numpy as jnp
from jax import lax
from jax.experimental import pallas as pl
from jax.experimental.pallas import tpu as pltpu
from jax.sharding import PartitionSpec as P

DH = 64
SCALE = DH ** -0.5
N_X = 4
N_CHIP = 16
WIDTH = 256
HALF = 512
MESH = pl.DeviceIdType.MESH
BF = jnp.bfloat16
F32 = jnp.float32


def dot(a, b):
    return jnp.dot(a, b, preferred_element_type=F32)


def dot_nt(a, b):
    return lax.dot_general(a, b, (((1,), (1,)), ((), ())), preferred_element_type=F32)


def flip(a):
    return a.astype(F32).T.astype(BF)


class Sems:
    def __init__(self, ref):
        self.ref, self.used = ref, 0

    def new(self):
        self.used += 1
        return self.ref.at[self.used - 1]


def kernel(
    frames, len_keys, len_values, w_query, w_key, w_value, w_out, cotangent,
    mixed_o, gframes_o, gwk_o, gwv_o, gw_o,
    fcols, frows, lens, len_t, wqf, wof, wo_p, wkv, cot,
    fpart, fpair, fsum, frs, fx, kpx, ff, kvp,
    q, ga, prob, att_t, att, gq_t, gq,
    mix_s, mix_r, gf_s, gf_r,
    gkv, gkv_pair, gkv_sum, gkv_rs, gkv_x, gkv_xr, gk16, m_s, m_r, gkm,
    w_s, w_pair, w_sum, w_ra, w_s2, w_rb, w_x, w_xr, w_f, w_ag, gwk_v, gwv_v, sem_ref,
):
    sems = Sems(sem_ref)
    me = lax.axis_index("ctx")
    x = lax.axis_index("head")
    core = lax.rem(me, 2)
    chip = lax.div(me, 2)
    other = me + 1 - 2 * core
    rows = frows.shape[0]
    step_a = 1 + 3 * core
    step_b = 4 - 3 * core
    at_a = lax.rem(lax.div(chip, step_a), N_X)
    at_b = lax.rem(lax.div(chip, step_b), N_X)

    def block(i, size):
        return pl.ds(pl.multiple_of(i * size, size), size)

    def beyond(o):
        return lax.rem(x + o, N_X)

    def piece(i):
        return block(i, 16)

    my_cols = block(x, WIDTH)
    my_rows = block(x, rows)
    mine = block(core, HALF)
    theirs = block(1 - core, HALF)
    hq = block(core, HALF)

    def load(src, dst):
        copy = pltpu.make_async_copy(src, dst, sems.new())
        copy.start()
        return copy

    in_f = [load(frames.at[:, my_cols], fcols), load(len_keys, lens.at[0]), load(len_values, lens.at[1])]
    in_w = [load(w_out.at[piece(chip), mine], wo_p.at[0])]
    in_k = [load(w_key, wkv.at[0]), load(w_value, wkv.at[1])]
    in_q = [load(frames.at[my_rows, :], frows), load(w_query, wqf.at[0])]
    in_c = [load(cotangent.at[my_rows, :], cot.at[:, my_cols])]

    barrier = pltpu.get_barrier_semaphore()
    pl.semaphore_signal(barrier, inc=1, device_id=(other, x), device_id_type=MESH)
    for dx in range(1, N_X):
        pl.semaphore_signal(barrier, inc=1, device_id=(me, beyond(dx)), device_id_type=MESH)

    @pl.loop(1, N_CHIP)
    def _(d):
        pl.semaphore_signal(
            barrier, inc=1, device_id=(lax.rem(me + 2 * d, 2 * N_CHIP), x), device_id_type=MESH
        )

    for copy in in_f:
        copy.wait()

    @pl.loop(0, 2)
    def _(t):
        fpart[t] = dot(lens[t], fcols[...]).astype(BF)

    pl.semaphore_wait(barrier, 1 + (N_X - 1) + (N_CHIP - 1))

    sent = []

    def landed(ref, sem):
        pltpu.make_async_copy(ref, ref, sem).wait()

    def remote(src, dst, s, r, device):
        pltpu.make_async_remote_copy(src, dst, s, r, device_id=device, device_id_type=MESH).start()

    def to_other(pairs, whole):
        s, r = sems.new(), sems.new()
        for src, dst in pairs:
            remote(src, dst, s, r, (other, x))
        sent.append((whole, s))
        return lambda: landed(whole, r)

    def to_x(src, dst, whole, which=(1, 3, 2)):
        s, r = sems.new(), sems.new()
        for dx in which:
            remote(src(dx), dst(N_X - dx), s, r, (me, beyond(dx)))
        sent.append((whole, s))
        return lambda: landed(whole, r)

    def to_chips(src, dst, whole):
        s, r = sems.new(), sems.new()

        @pl.loop(1, N_CHIP)
        def _(d):
            peer = lax.rem(chip + d, N_CHIP)
            remote(src(peer), dst(N_CHIP - d), s, r, (2 * peer + core, x))

        sent.append((whole, s))
        return lambda: landed(whole, r)

    def to_line(src, dst, whole, at, step):
        s, r = sems.new(), sems.new()
        for d in (1, 3, 2):
            peer = lax.rem(at + d, N_X)
            remote(src(peer), dst(N_X - d), s, r, (me + 2 * step * (peer - at), x))
        sent.append((whole, s))
        return lambda: landed(whole, r)

    def gather(src, full, fifteen):
        copy = load(src, full)
        done = to_chips(lambda j: src, lambda o: full, fifteen)

        def arrive():
            copy.wait()
            done()

        return arrive

    def add(first, slots, count):
        total = first.astype(F32)
        for o in range(1, count):
            total = total + slots(o).astype(F32)
        return total.astype(BF)

    got_f = to_other([(fpart.at[1 - core], fpair)], fpair)
    got_wo = to_x(lambda dx: w_out.at[piece(chip), mine], lambda o: wo_p.at[o], wo_p.at[1:N_X])
    got_wq = to_x(
        lambda dx: w_query.at[hq, :], lambda o: wqf.at[o, hq, :], wqf.at[0:2, 0:HALF, :], (1, 3)
    )

    @pl.loop(0, 2)
    def _(t):
        @pl.loop(0, 4)
        def _(b):
            at = block(b, 512)
            len_t[t, at, :] = flip(lens[t, :, at])

    got_f()
    fsum[...] = (fpart[core].astype(F32) + fpair[...].astype(F32)).astype(BF)
    got_frs = to_chips(lambda j: fsum.at[piece(j), :], lambda o: frs.at[o], frs.at[1:N_CHIP])
    for copy in in_w:
        copy.wait()
    got_wo()
    got_wof = gather(wo_p, wof.at[:, piece(chip), mine], wof.at[:, 0:240, 0:HALF])
    for copy in in_k + in_q:
        copy.wait()
    got_frs()
    fx[0] = add(fsum[piece(chip), :], lambda o: frs[o], N_CHIP)
    got_fx = to_x(lambda dx: fx.at[0], lambda o: fx.at[o], fx.at[1:N_X])
    q[0] = dot(frows[...], wqf[0]).astype(BF)
    got_fx()
    total = dot(fx[0], wkv[core, my_cols, :])
    for o in range(1, N_X):
        total = total + dot(fx[o], wkv[core, block(beyond(o), WIDTH), :])
    kpx[0] = total.astype(BF)
    got_kpx = to_x(lambda dx: kpx.at[0], lambda o: kpx.at[o], kpx.at[1:N_X])
    got_wq2 = to_x(lambda dx: w_query.at[hq, :], lambda o: wqf.at[o, hq, :], wqf.at[0, 0:HALF, :], (2,))
    got_cot = to_x(
        lambda dx: cotangent.at[block(beyond(dx), rows), :],
        lambda o: cot.at[:, my_cols],
        cot.at[:, 0 : 3 * WIDTH],
    )
    got_kpx()
    got_kvp = gather(kpx, kvp.at[core, :, piece(chip), :], kvp.at[0, :, 0:240, :])

    got_wq()
    got_wqo = to_other([(wqf.at[o, hq, :], wqf.at[o, hq, :]) for o in (1, 3)], wqf.at[0:2, 0:HALF, :])
    got_wqo()
    for o in (1, 3):
        q[o] = dot(frows[...], wqf[o]).astype(BF)
    got_wof()
    got_woo = to_other([(wof.at[:, :, mine], wof.at[:, :, mine])], wof.at[:, :, 0:HALF])
    got_kvp()
    got_kvo = to_other([(kvp.at[core], kvp.at[core])], kvp.at[0])
    got_ff = gather(fx, ff.at[core, :, piece(chip), :], ff.at[0, :, 0:240, :])
    got_wq2()
    got_wqo2 = to_other([(wqf.at[2, hq, :], wqf.at[2, hq, :])], wqf.at[0, 0:HALF, :])
    got_wqo2()
    q[2] = dot(frows[...], wqf[2]).astype(BF)
    got_kvo()

    lane = lax.broadcasted_iota(jnp.int32, (WIDTH, WIDTH), 1) // DH

    def only(h, a):
        return jnp.where(lane == h, a.astype(F32), 0.0).astype(BF)

    @pl.loop(0, N_X)
    def _(g):
        kg = kvp[0, g]
        vg_t = flip(kvp[1, g])
        qg = q[g]
        for h in range(4):
            scores = dot_nt(only(h, kg), qg)
            top = jnp.max(scores, axis=0, keepdims=True)
            e = jnp.exp((scores - top) * SCALE)
            p = (e * (1.0 / jnp.sum(e, axis=0, keepdims=True))).astype(BF)
            prob[4 * g + h] = p
            att_t[g, h * DH : (h + 1) * DH, :] = dot(vg_t[h * DH : (h + 1) * DH, :], p).astype(BF)
        att[g] = flip(att_t[g])

    got_woo()

    @pl.loop(0, N_X)
    def _(n):
        at = block(beyond(n), WIDTH)
        heads = jnp.concatenate([att[o] for o in range(N_X)], axis=1)
        weights = jnp.concatenate([wof[o, :, at] for o in range(N_X)], axis=0)
        mix_s[n] = dot(heads, weights).astype(BF)

    got_mix = to_x(lambda dx: mix_s.at[dx], lambda o: mix_r.at[my_rows, :], mix_r.at[0 : 3 * rows, :])
    own_mix = load(mix_s.at[0], mix_r.at[my_rows, :])

    for copy in in_c:
        copy.wait()
    got_cot()

    @pl.loop(0, N_X)
    def _(g):
        w_s[0, g] = dot(att_t[g], cot[...]).astype(BF)

    got_wpair = [to_other([(w_s.at[0, :, :, theirs], w_pair.at[0])], w_pair.at[0])]

    @pl.loop(0, N_X)
    def _(g):
        ga[g] = dot_nt(cot[...], wof[g]).astype(BF)

    def stage_a(k):
        got_wpair[k]()

        @pl.loop(0, N_X)
        def _(g):
            w_sum[k, g] = (w_s[k, g, :, mine].astype(F32) + w_pair[k, g].astype(F32)).astype(BF)

        return to_line(
            lambda p: w_sum.at[k, :, block(p, 64), :], lambda o: w_ra.at[k, o], w_ra.at[k, 1:N_X], at_a, step_a
        )

    def stage_b(k):
        got_wa[k]()

        @pl.loop(0, N_X)
        def _(g):
            w_s2[k, g] = add(w_sum[k, g, block(at_a, 64), :], lambda o: w_ra[k, o, g], N_X)

        return to_line(
            lambda p: w_s2.at[k, :, piece(p), :], lambda o: w_rb.at[k, o], w_rb.at[k, 1:N_X], at_b, step_b
        )

    def stage_x(k):
        got_wb[k]()
        w_x[k] = add(w_s2[k, :, piece(at_b), :], lambda o: w_rb[k, o], N_X)
        return to_x(lambda dx: w_x.at[k, dx], lambda o: w_xr.at[k, o], w_xr.at[k, 1:N_X])

    def stage_w(k):
        got_wx[k]()
        w_f[k] = add(w_x[k, 0], lambda o: w_xr[k, o], N_X)
        return gather(w_f.at[k], w_ag.at[k, core, piece(4 * at_a + at_b), :], w_ag.at[k, 0, 0:240, :])

    got_wa = [stage_a(0)]
    got_ff()
    got_ffo = to_other([(ff.at[core], ff.at[core])], ff.at[0])

    def backward(g):
        vg = kvp[1, g]
        kg_t = flip(kvp[0, g])
        qg = q[g]
        gag = ga[g]
        gk = jnp.zeros((WIDTH, WIDTH), F32)
        gv = jnp.zeros((WIDTH, WIDTH), F32)
        for h in range(4):
            pb = prob[4 * g + h]
            p = pb.astype(F32)
            gp = dot_nt(only(h, vg), gag)
            inner = jnp.sum(p * gp, axis=0, keepdims=True)
            gs = (p * (gp - inner) * SCALE).astype(BF)
            gq_t[g, h * DH : (h + 1) * DH, :] = dot(kg_t[h * DH : (h + 1) * DH, :], gs).astype(BF)
            gk = jnp.where(lane == h, dot(gs, qg), gk)
            gv = jnp.where(lane == h, dot(pb, gag), gv)
        gkv[0, g] = gk.astype(BF)
        gkv[1, g] = gv.astype(BF)
        gq[g] = flip(gq_t[g])

    pl.loop(0, 3)(backward)
    got_wb = [stage_b(0)]
    pl.loop(3, N_X)(backward)

    got_gpair = to_other([(gkv.at[1 - core], gkv_pair)], gkv_pair)

    @pl.loop(0, N_X)
    def _(g):
        w_s[1, g] = dot(gq_t[g], frows[...]).astype(BF)

    got_wpair.append(to_other([(w_s.at[1, :, :, theirs], w_pair.at[1])], w_pair.at[1]))
    got_gpair()

    @pl.loop(0, N_X)
    def _(g):
        gkv_sum[g] = (gkv[core, g].astype(F32) + gkv_pair[g].astype(F32)).astype(BF)

    got_grs = to_chips(lambda j: gkv_sum.at[:, piece(j), :], lambda o: gkv_rs.at[o], gkv_rs.at[1:N_CHIP])
    got_wx = [stage_x(0)]
    got_wa.append(stage_a(1))

    @pl.loop(0, N_X)
    def _(n):
        at = block(beyond(n), WIDTH)
        heads = jnp.concatenate([gq[o] for o in range(N_X)], axis=1)
        weights = jnp.concatenate([wqf[o, at, :] for o in range(N_X)], axis=1)
        gf_s[n] = dot_nt(heads, weights).astype(BF)

    def send_gf(which):
        return to_x(
            lambda dx: gf_s.at[dx], lambda o: gf_r.at[my_rows, :], gf_r.at[0 : len(which) * rows, :], which
        )

    got_gf = [send_gf((1, 3))]
    own_gf = load(gf_s.at[0], gf_r.at[my_rows, :])

    got_grs()
    gkv_x[...] = add(gkv_sum[:, piece(chip), :], lambda o: gkv_rs[o], N_CHIP)
    got_gx = to_x(lambda dx: gkv_x.at[dx], lambda o: gkv_xr.at[o], gkv_xr.at[1:N_X])
    got_w = [stage_w(0)]
    got_gx()
    gk16[0] = add(gkv_x[0], lambda o: gkv_xr[o], N_X)
    for o in range(N_X):
        m_s[o] = dot_nt(gk16[0], wkv[core, block(beyond(o), WIDTH), :]).astype(BF)
    got_m = to_x(lambda dx: m_s.at[dx], lambda o: m_r.at[o], m_r.at[1:N_X])
    got_gf.append(send_gf((2,)))
    got_m()
    gk16[1] = add(m_s[0], lambda o: m_r[o], N_X)
    got_gkm = gather(gk16, gkm.at[core, :, piece(chip), :], gkm.at[0, :, 0:240, :])
    got_wb.append(stage_b(1))
    got_w[0]()
    got_wo2 = [to_other([(w_ag.at[0, core], w_ag.at[0, core])], w_ag.at[0, 0])]
    outs = []
    own_mix.wait()
    got_mix()
    outs.append(load(mix_r, mixed_o))
    got_wx.append(stage_x(1))
    got_gkm()
    got_gkmo = to_other([(gkm.at[core], gkm.at[core])], gkm.at[0])
    got_w.append(stage_w(1))
    got_ffo()
    got_gkmo()

    @pl.loop(0, N_X)
    def _(o):
        at = block(beyond(o), WIDTH)
        gwk_v[at, :] = dot(flip(ff[0, o]), gkm[0, 0]).astype(BF)
        gwv_v[at, :] = dot(flip(ff[1, o]), gkm[1, 0]).astype(BF)

    outs.append(load(gwk_v, gwk_o))
    outs.append(load(gwv_v, gwv_o))
    own_gf.wait()
    for wait in got_gf:
        wait()

    @pl.loop(0, N_X)
    def _(b):
        at = block(b, rows)
        total = gf_r[at, :].astype(F32) + dot(len_t[0, at, :], gkm[0, 1]) + dot(len_t[1, at, :], gkm[1, 1])
        gf_r[at, :] = total.astype(BF)

    outs.append(load(gf_r, gframes_o))
    got_wo2[0]()
    outs.append(load(w_ag.at[0], gw_o.at[0]))
    got_w[1]()
    got_wo2.append(to_other([(w_ag.at[1, core], w_ag.at[1, core])], w_ag.at[1, 0]))
    got_wo2[1]()
    outs.append(load(w_ag.at[1], gw_o.at[1]))
    for ref, sem in sent:
        landed(ref, sem)
    for copy in outs:
        copy.wait()


def finish(
    mixed, gframes, gwk, gwv, gw,
    mixed_o, gframes_o, gwq_o, gwk_o, gwv_o, gwo_o,
    raw_k, raw_w, raw_f, wide, wide_o, sem_ref,
):
    sems = Sems(sem_ref)

    def copy(src, dst):
        c = pltpu.make_async_copy(src, dst, sems.new())
        c.start()
        return c

    ins = [copy(gwk, raw_k.at[0]), copy(gwv, raw_k.at[1]), copy(gw.at[0], raw_w.at[0]), copy(gw.at[1], raw_w.at[1])]
    through = [copy(mixed, raw_f.at[0]), copy(gframes, raw_f.at[1])]
    outs = []
    for k, out in enumerate((gwk_o, gwv_o)):
        ins[k].wait()
        wide[k] = raw_k[k].astype(F32)
        outs.append(copy(wide.at[k], out))
    for k, out in enumerate((mixed_o, gframes_o)):
        through[k].wait()
        outs.append(copy(raw_f.at[k], out))
    ins[2].wait()
    for t in range(2):
        wide_o[:, t * HALF : (t + 1) * HALF] = raw_w[0, t].astype(F32)
    outs.append(copy(wide_o, gwo_o))
    ins[3].wait()
    for t in range(2):
        wide[2, t * HALF : (t + 1) * HALF, :] = raw_w[1, t].astype(F32).T
    outs.append(copy(wide.at[2], gwq_o))
    for c in outs:
        c.wait()


def body(frames, len_keys, len_values, w_query, w_key, w_value, w_out, cotangent):
    span, depth = frames.shape
    rows = span // N_X

    def bf(*shape):
        return pltpu.VMEM(shape, BF)

    scratch = [
        bf(span, 256), bf(rows, depth), bf(2, 256, span), bf(2, span, 256),
        bf(4, 1024, 256), bf(4, 256, 1024), bf(4, 16, 512), bf(2, 1024, 256), bf(rows, depth),
        bf(2, 256, 256), bf(256, 256), bf(256, 256), bf(16, 16, 256),
        bf(4, 16, 256), bf(4, 16, 256), bf(2, 4, 256, 256), bf(2, 4, 256, 256),
        bf(4, rows, 256), bf(4, rows, 256), bf(16, 256, rows),
        bf(4, 256, rows), bf(4, rows, 256), bf(4, 256, rows), bf(4, rows, 256),
        bf(4, rows, 256), bf(span, 256), bf(4, rows, 256), bf(span, 256),
        bf(2, 4, 256, 256), bf(4, 256, 256), bf(4, 256, 256), bf(16, 4, 16, 256),
        bf(4, 16, 256), bf(4, 16, 256), bf(2, 16, 256), bf(4, 16, 256), bf(4, 16, 256),
        bf(2, 2, 256, 256),
        bf(2, 4, 256, 1024), bf(2, 4, 256, 512), bf(2, 4, 256, 512), bf(2, 4, 4, 64, 512),
        bf(2, 4, 64, 512), bf(2, 4, 4, 16, 512), bf(2, 4, 16, 512), bf(2, 4, 16, 512),
        bf(2, 16, 512), bf(2, 2, 256, 512), bf(depth, 256), bf(depth, 256),
        pltpu.SemaphoreType.DMA((100,)),
    ]
    any_ = pl.BlockSpec(memory_space=pl.ANY)
    shape = jax.ShapeDtypeStruct
    raw = pl.pallas_call(
        kernel,
        out_shape=(
            shape((span, 256), BF), shape((span, 256), BF),
            shape((depth, 256), BF), shape((depth, 256), BF), shape((2, 2, 256, 512), BF),
        ),
        in_specs=[any_] * 8,
        out_specs=(any_,) * 5,
        scratch_shapes=scratch,
        compiler_params=pltpu.CompilerParams(
            collective_id=0, has_side_effects=True, vmem_limit_bytes=60 * 1024 * 1024
        ),
        cost_estimate=pl.CostEstimate(flops=14_000_000_000, bytes_accessed=24_000_000, transcendentals=2_097_152),
    )(frames, len_keys, len_values, w_query, w_key, w_value, w_out, cotangent)
    return pl.pallas_call(
        finish,
        out_shape=(
            shape((span, 256), BF), shape((span, 256), BF),
            shape((depth, 256), F32), shape((depth, 256), F32), shape((depth, 256), F32), shape((256, depth), F32),
        ),
        in_specs=[any_] * 5,
        out_specs=(any_,) * 6,
        scratch_shapes=[
            bf(2, depth, 256), bf(2, 2, 256, 512), bf(2, span, 256),
            pltpu.VMEM((3, depth, 256), F32), pltpu.VMEM((256, depth), F32),
            pltpu.SemaphoreType.DMA((12,)),
        ],
        compiler_params=pltpu.CompilerParams(vmem_limit_bytes=60 * 1024 * 1024),
        cost_estimate=pl.CostEstimate(flops=1_000_000, bytes_accessed=11_000_000, transcendentals=0),
    )(*raw)


def solution(mesh):
    placed = (
        P("ctx", None),
        P(None, "ctx"),
        P(None, "ctx"),
        P(None, "head"),
        P(None, "head"),
        P(None, "head"),
        P("head", None),
        P("ctx", "head"),
    )
    return jax.shard_map(
        body,
        mesh=mesh,
        in_specs=placed,
        out_specs=(
            P("ctx", "head"),
            P("ctx", "head"),
            P(None, "head"),
            P(None, "head"),
            P(None, "head"),
            P("head", None),
        ),
        check_vma=False,
    )
```

time: 634 us -> 110 us (0.17)
  blocking collectives: 258 us -> 0 us
  waiting for transfers between devices: 254 us -> 0 us
  Pallas kernels: 0 us -> 109 us
  matrix products: 92.3 us -> 0 us
  between operations: 14 us -> 0.64 us
  local copies, waits for them, and re-layouts: 9.12 us -> 0 us
    psum x2 -> x0, blocking collectives: 258 us -> none  [the longest x1 130 us: body(): keys_sum, values_sum = lax.psum((keys_part, values_part), 'ctx')]
    reduce_scatter x2 -> x0, waiting for transfers between devices: 155 us -> none  [the longest x1 79.9 us: body(): lax.psum_scatter(frame_terms, 'head', scatter_dimension=1, tiled=True)]
    pallas_call x0 -> x2, Pallas kernels: none -> 109 us  [the longest x1 105 us: body(): pl.pallas_call(kernel, out_shape=(shape((span, 256), BF), shape((span, 25...]
    psum x1 -> x0, waiting for transfers between devices: 98.8 us -> none  [body(): lax.psum((wq_part, wk_part, wv_part, grad_wo_part), 'ctx')]
    dot_general x19 -> x0, matrix products: 87.4 us -> none  [the longest x1 14.8 us: body(): jnp.einsum('hsk,khd->shd', grad_score, keys_proj, preferred_element_type=...]
    unnamed x30 -> x0, local copies, waits for them, and re-layouts: 9.12 us -> none
  transfers between devices with their start and end apart: 4 -> 0, of which waited for: 3 -> 0; matrix products, arithmetic and copies ran while one was open for 7% -> 0% of each run, Pallas kernels for 0% -> 0%
where the time goes in v2:
time: 110 us
  Pallas kernels  109 us (99%)
    pallas_call x1, Pallas kernels, body(): pl.pallas_call(kernel, out_shape=(shape((span, 256), BF), shape((span, 25...  105 us
    pallas_call x1, Pallas kernels, body(): pl.pallas_call(finish, out_shape=(shape((span, 256), BF), shape((span, 25...  4.25 us

profile of v2, /device:TPU:1, one launch (start us, length us, event | category | flops | bytes accessed | tf_op | source)
XLA Modules:
  0.0 110.0 jit_solution(10109020928550229777)
XLA Ops:
  0.6 105.1 %shard_map.127 = (bf16[2048,256]{1,0:T(8,128)(2,1)}, bf16[2048,256]{1,0:T(8,128)(2,1)}, bf16[1024,256]{1,0:T(8,128)(2,1)}, bf16[1024,256]{1,0:T(8,128)(2,1)}, bf16[2,2,256,512]{3,2,1,0:T(8,128)(2,1)}) custom-call(bf16[2048,1024]{1,0:T(8,128)(2,1)} %frames.1, bf16[256,2048]{1,0:T(8,128)(2,1)} %len_keys.1, bf16[256,2048]{1,0:T(8,128)(2,1)} %len_values.1, ...), custom_call_target="tpu_custom_call" | custom-call | flops 14000000000 | bytes 24000000 | tf_op jit(solution)/shard_map/pallas_call | solution.py:476
  105.7 4.2 %shard_map.128 = (bf16[2048,256]{1,0:T(8,128)(2,1)}, bf16[2048,256]{1,0:T(8,128)(2,1)}, f32[1024,256]{1,0:T(8,128)}, f32[1024,256]{1,0:T(8,128)}, f32[1024,256]{1,0:T(8,128)}, /*index=5*/f32[256,1024]{1,0:T(8,128)}) custom-call(bf16[2048,256]{1,0:T(8,128)(2,1)} %get-tuple-element.11.mixed, bf16[2048,256]{1,0:T(8,128)(2,1)} %get-tuple-element.12.gframes, ...), custom_call_target="tpu_custom_call" | custom-call | flops 1000000 | bytes 11000000 | tf_op jit(solution)/shard_map/pallas_call | solution.py:490

commit v3 on v2

--- a/solution.py
+++ b/solution.py
@@ -194,6 +194,7 @@
         total = total + dot(fx[o], wkv[core, block(beyond(o), WIDTH), :])
     kpx[0] = total.astype(BF)
     got_kpx = to_x(lambda dx: kpx.at[0], lambda o: kpx.at[o], kpx.at[1:N_X])
+    got_k = {0: gather(kpx.at[0], kvp.at[core, 0, piece(chip), :], kvp.at[0, 0, 0:240, :])}
     got_wq2 = to_x(lambda dx: w_query.at[hq, :], lambda o: wqf.at[o, hq, :], wqf.at[0, 0:HALF, :], (2,))
     got_cot = to_x(
         lambda dx: cotangent.at[block(beyond(dx), rows), :],
@@ -201,31 +202,26 @@
         cot.at[:, 0 : 3 * WIDTH],
     )
     got_kpx()
-    got_kvp = gather(kpx, kvp.at[core, :, piece(chip), :], kvp.at[0, :, 0:240, :])
+    for o in (1, 3, 2):
+        got_k[o] = gather(kpx.at[o], kvp.at[core, o, piece(chip), :], kvp.at[0, o, 0:240, :])
 
     got_wq()
     got_wqo = to_other([(wqf.at[o, hq, :], wqf.at[o, hq, :]) for o in (1, 3)], wqf.at[0:2, 0:HALF, :])
     got_wqo()
     for o in (1, 3):
         q[o] = dot(frows[...], wqf[o]).astype(BF)
-    got_wof()
-    got_woo = to_other([(wof.at[:, :, mine], wof.at[:, :, mine])], wof.at[:, :, 0:HALF])
-    got_kvp()
-    got_kvo = to_other([(kvp.at[core], kvp.at[core])], kvp.at[0])
-    got_ff = gather(fx, ff.at[core, :, piece(chip), :], ff.at[0, :, 0:240, :])
-    got_wq2()
-    got_wqo2 = to_other([(wqf.at[2, hq, :], wqf.at[2, hq, :])], wqf.at[0, 0:HALF, :])
-    got_wqo2()
-    q[2] = dot(frows[...], wqf[2]).astype(BF)
-    got_kvo()
+    got_kvo = {}
+
+    def pass_on(o):
+        got_k[o]()
+        got_kvo[o] = to_other([(kvp.at[core, o], kvp.at[core, o])], kvp.at[0, o])
 
     lane = lax.broadcasted_iota(jnp.int32, (WIDTH, WIDTH), 1) // DH
 
     def only(h, a):
         return jnp.where(lane == h, a.astype(F32), 0.0).astype(BF)
 
-    @pl.loop(0, N_X)
-    def _(g):
+    def forward(g):
         kg = kvp[0, g]
         vg_t = flip(kvp[1, g])
         qg = q[g]
@@ -238,6 +234,25 @@
             att_t[g, h * DH : (h + 1) * DH, :] = dot(vg_t[h * DH : (h + 1) * DH, :], p).astype(BF)
         att[g] = flip(att_t[g])
 
+    pass_on(0)
+    got_kvo[0]()
+    forward(0)
+    pass_on(1)
+    got_wq2()
+    got_wqo2 = to_other([(wqf.at[2, hq, :], wqf.at[2, hq, :])], wqf.at[0, 0:HALF, :])
+    got_wof()
+    got_woo = to_other([(wof.at[:, :, mine], wof.at[:, :, mine])], wof.at[:, :, 0:HALF])
+    pass_on(3)
+    got_kvo[1]()
+    forward(1)
+    pass_on(2)
+    got_ff = gather(fx, ff.at[core, :, piece(chip), :], ff.at[0, :, 0:240, :])
+    got_kvo[3]()
+    forward(3)
+    got_wqo2()
+    q[2] = dot(frows[...], wqf[2]).astype(BF)
+    got_kvo[2]()
+    forward(2)
     got_woo()
 
     @pl.loop(0, N_X)
@@ -254,33 +269,36 @@
         copy.wait()
     got_cot()
 
-    @pl.loop(0, N_X)
-    def _(g):
-        w_s[0, g] = dot(att_t[g], cot[...]).astype(BF)
-
-    got_wpair = [to_other([(w_s.at[0, :, :, theirs], w_pair.at[0])], w_pair.at[0])]
+    got_wpair, got_wa = ({}, {}), ({}, {})
+
+    def to_pair(k, o):
+        got_wpair[k][o] = to_other([(w_s.at[k, o, :, theirs], w_pair.at[k, o])], w_pair.at[k, o])
+
+    def stage_a(k, o):
+        got_wpair[k][o]()
+        w_sum[k, o] = (w_s[k, o, :, mine].astype(F32) + w_pair[k, o].astype(F32)).astype(BF)
+        got_wa[k][o] = to_line(
+            lambda p: w_sum.at[k, o, block(p, 64), :], lambda d: w_ra.at[k, o, d], w_ra.at[k, o, 1:N_X], at_a, step_a
+        )
+
+    for o in range(N_X):
+        w_s[0, o] = dot(att_t[o], cot[...]).astype(BF)
+        to_pair(0, o)
 
     @pl.loop(0, N_X)
     def _(g):
         ga[g] = dot_nt(cot[...], wof[g]).astype(BF)
 
-    def stage_a(k):
-        got_wpair[k]()
+    for o in range(N_X):
+        stage_a(0, o)
+
+    def stage_b(k):
+        for o in range(N_X):
+            got_wa[k][o]()
 
         @pl.loop(0, N_X)
         def _(g):
-            w_sum[k, g] = (w_s[k, g, :, mine].astype(F32) + w_pair[k, g].astype(F32)).astype(BF)
-
-        return to_line(
-            lambda p: w_sum.at[k, :, block(p, 64), :], lambda o: w_ra.at[k, o], w_ra.at[k, 1:N_X], at_a, step_a
-        )
-
-    def stage_b(k):
-        got_wa[k]()
-
-        @pl.loop(0, N_X)
-        def _(g):
-            w_s2[k, g] = add(w_sum[k, g, block(at_a, 64), :], lambda o: w_ra[k, o, g], N_X)
+            w_s2[k, g] = add(w_sum[k, g, block(at_a, 64), :], lambda o: w_ra[k, g, o], N_X)
 
         return to_line(
             lambda p: w_s2.at[k, :, piece(p), :], lambda o: w_rb.at[k, o], w_rb.at[k, 1:N_X], at_b, step_b
@@ -296,7 +314,6 @@
         w_f[k] = add(w_x[k, 0], lambda o: w_xr[k, o], N_X)
         return gather(w_f.at[k], w_ag.at[k, core, piece(4 * at_a + at_b), :], w_ag.at[k, 0, 0:240, :])
 
-    got_wa = [stage_a(0)]
     got_ff()
     got_ffo = to_other([(ff.at[core], ff.at[core])], ff.at[0])
 
@@ -320,26 +337,37 @@
         gkv[1, g] = gv.astype(BF)
         gq[g] = flip(gq_t[g])
 
-    pl.loop(0, 3)(backward)
-    got_wb = [stage_b(0)]
-    pl.loop(3, N_X)(backward)
-
-    got_gpair = to_other([(gkv.at[1 - core], gkv_pair)], gkv_pair)
-
-    @pl.loop(0, N_X)
-    def _(g):
-        w_s[1, g] = dot(gq_t[g], frows[...]).astype(BF)
-
-    got_wpair.append(to_other([(w_s.at[1, :, :, theirs], w_pair.at[1])], w_pair.at[1]))
-    got_gpair()
-
-    @pl.loop(0, N_X)
-    def _(g):
-        gkv_sum[g] = (gkv[core, g].astype(F32) + gkv_pair[g].astype(F32)).astype(BF)
-
-    got_grs = to_chips(lambda j: gkv_sum.at[:, piece(j), :], lambda o: gkv_rs.at[o], gkv_rs.at[1:N_CHIP])
+    order = (1, 2, 3, 0)
+    got_gpair, got_grs, got_gx = {}, {}, {}
+
+    def pair_sums(o):
+        got_gpair[o]()
+        gkv_sum[o] = (gkv[core, o].astype(F32) + gkv_pair[o].astype(F32)).astype(BF)
+        got_grs[o] = to_chips(
+            lambda j: gkv_sum.at[o, piece(j), :], lambda d: gkv_rs.at[o, d], gkv_rs.at[o, 1:N_CHIP]
+        )
+        stage_a(1, o)
+
+    def chip_sums(o):
+        got_grs[o]()
+        gkv_x[o] = add(gkv_sum[o, piece(chip), :], lambda d: gkv_rs[o, d], N_CHIP)
+        if o:
+            got_gx[o] = to_x(lambda dx: gkv_x.at[dx], lambda d: gkv_xr.at[d], gkv_xr.at[N_X - o], (o,))
+
+    for i, o in enumerate(order):
+        backward(o)
+        got_gpair[o] = to_other([(gkv.at[1 - core, o], gkv_pair.at[o])], gkv_pair.at[o])
+        w_s[1, o] = dot(gq_t[o], frows[...]).astype(BF)
+        to_pair(1, o)
+        if i > 0:
+            pair_sums(order[i - 1])
+        if i > 1:
+            chip_sums(order[i - 2])
+        if i == 2:
+            got_wb = [stage_b(0)]
+    pair_sums(order[3])
+    chip_sums(order[2])
     got_wx = [stage_x(0)]
-    got_wa.append(stage_a(1))
 
     @pl.loop(0, N_X)
     def _(n):
@@ -356,30 +384,29 @@
     got_gf = [send_gf((1, 3))]
     own_gf = load(gf_s.at[0], gf_r.at[my_rows, :])
 
-    got_grs()
-    gkv_x[...] = add(gkv_sum[:, piece(chip), :], lambda o: gkv_rs[o], N_CHIP)
-    got_gx = to_x(lambda dx: gkv_x.at[dx], lambda o: gkv_xr.at[o], gkv_xr.at[1:N_X])
-    got_w = [stage_w(0)]
-    got_gx()
+    chip_sums(0)
+    for o in (1, 2, 3):
+        got_gx[o]()
     gk16[0] = add(gkv_x[0], lambda o: gkv_xr[o], N_X)
     for o in range(N_X):
         m_s[o] = dot_nt(gk16[0], wkv[core, block(beyond(o), WIDTH), :]).astype(BF)
     got_m = to_x(lambda dx: m_s.at[dx], lambda o: m_r.at[o], m_r.at[1:N_X])
-    got_gf.append(send_gf((2,)))
+    got_w = [stage_w(0)]
+    got_wb.append(stage_b(1))
     got_m()
     gk16[1] = add(m_s[0], lambda o: m_r[o], N_X)
     got_gkm = gather(gk16, gkm.at[core, :, piece(chip), :], gkm.at[0, :, 0:240, :])
-    got_wb.append(stage_b(1))
-    got_w[0]()
-    got_wo2 = [to_other([(w_ag.at[0, core], w_ag.at[0, core])], w_ag.at[0, 0])]
+    got_wx.append(stage_x(1))
+    got_gf.append(send_gf((2,)))
     outs = []
     own_mix.wait()
     got_mix()
     outs.append(load(mix_r, mixed_o))
-    got_wx.append(stage_x(1))
+    got_w[0]()
+    got_wo2 = [to_other([(w_ag.at[0, core], w_ag.at[0, core])], w_ag.at[0, 0])]
+    got_w.append(stage_w(1))
     got_gkm()
     got_gkmo = to_other([(gkm.at[core], gkm.at[core])], gkm.at[0])
-    got_w.append(stage_w(1))
     got_ffo()
     got_gkmo()
 
@@ -463,13 +490,13 @@
         bf(4, rows, 256), bf(4, rows, 256), bf(16, 256, rows),
         bf(4, 256, rows), bf(4, rows, 256), bf(4, 256, rows), bf(4, rows, 256),
         bf(4, rows, 256), bf(span, 256), bf(4, rows, 256), bf(span, 256),
-        bf(2, 4, 256, 256), bf(4, 256, 256), bf(4, 256, 256), bf(16, 4, 16, 256),
+        bf(2, 4, 256, 256), bf(4, 256, 256), bf(4, 256, 256), bf(4, 16, 16, 256),
         bf(4, 16, 256), bf(4, 16, 256), bf(2, 16, 256), bf(4, 16, 256), bf(4, 16, 256),
         bf(2, 2, 256, 256),
         bf(2, 4, 256, 1024), bf(2, 4, 256, 512), bf(2, 4, 256, 512), bf(2, 4, 4, 64, 512),
         bf(2, 4, 64, 512), bf(2, 4, 4, 16, 512), bf(2, 4, 16, 512), bf(2, 4, 16, 512),
         bf(2, 16, 512), bf(2, 2, 256, 512), bf(depth, 256), bf(depth, 256),
-        pltpu.SemaphoreType.DMA((100,)),
+        pltpu.SemaphoreType.DMA((180,)),
     ]
     any_ = pl.BlockSpec(memory_space=pl.ANY)
     shape = jax.ShapeDtypeStruct

time: 110 us -> 101 us (0.918)
  Pallas kernels: 109 us -> 100 us
    pallas_call x1, Pallas kernels: 105 us -> 95.7 us  [body(): pl.pallas_call(kernel, out_shape=(shape((span, 256), BF), shape((span, 25...]
where the time goes in v3:
time: 101 us
  Pallas kernels  100 us (99%)
    pallas_call x1, Pallas kernels, body(): pl.pallas_call(kernel, out_shape=(shape((span, 256), BF), shape((span, 25...  95.7 us
    pallas_call x1, Pallas kernels, body(): pl.pallas_call(finish, out_shape=(shape((span, 256), BF), shape((span, 25...  4.25 us

profile of v3, /device:TPU:1, one launch (start us, length us, event | category | flops | bytes accessed | tf_op | source)
XLA Modules:
  0.0 100.8 jit_solution(917092239415017730)
XLA Ops:
  0.6 95.7 %shard_map.127 = (bf16[2048,256]{1,0:T(8,128)(2,1)}, bf16[2048,256]{1,0:T(8,128)(2,1)}, bf16[1024,256]{1,0:T(8,128)(2,1)}, bf16[1024,256]{1,0:T(8,128)(2,1)}, bf16[2,2,256,512]{3,2,1,0:T(8,128)(2,1)}) custom-call(bf16[2048,1024]{1,0:T(8,128)(2,1)} %frames.1, bf16[256,2048]{1,0:T(8,128)(2,1)} %len_keys.1, bf16[256,2048]{1,0:T(8,128)(2,1)} %len_values.1, ...), custom_call_target="tpu_custom_call" | custom-call | flops 14000000000 | bytes 24000000 | tf_op jit(solution)/shard_map/pallas_call | solution.py:503
  96.4 4.2 %shard_map.128 = (bf16[2048,256]{1,0:T(8,128)(2,1)}, bf16[2048,256]{1,0:T(8,128)(2,1)}, f32[1024,256]{1,0:T(8,128)}, f32[1024,256]{1,0:T(8,128)}, f32[1024,256]{1,0:T(8,128)}, /*index=5*/f32[256,1024]{1,0:T(8,128)}) custom-call(bf16[2048,256]{1,0:T(8,128)(2,1)} %get-tuple-element.11.mixed, bf16[2048,256]{1,0:T(8,128)(2,1)} %get-tuple-element.12.gframes, ...), custom_call_target="tpu_custom_call" | custom-call | flops 1000000 | bytes 11000000 | tf_op jit(solution)/shard_map/pallas_call | solution.py:517

commit v4 on v3

--- a/solution.py
+++ b/solution.py
@@ -80,7 +80,7 @@
         return copy
 
     in_f = [load(frames.at[:, my_cols], fcols), load(len_keys, lens.at[0]), load(len_values, lens.at[1])]
-    in_w = [load(w_out.at[piece(chip), mine], wo_p.at[0])]
+    in_w = [load(w_out, wof.at[0])]
     in_k = [load(w_key, wkv.at[0]), load(w_value, wkv.at[1])]
     in_q = [load(frames.at[my_rows, :], frows), load(w_query, wqf.at[0])]
     in_c = [load(cotangent.at[my_rows, :], cot.at[:, my_cols])]
@@ -178,10 +178,12 @@
     got_f()
     fsum[...] = (fpart[core].astype(F32) + fpair[...].astype(F32)).astype(BF)
     got_frs = to_chips(lambda j: fsum.at[piece(j), :], lambda o: frs.at[o], frs.at[1:N_CHIP])
+    got_wo()
+    got_wof = gather(
+        wo_p.at[1:N_X], wof.at[1:N_X, piece(chip), mine], wof.at[1:N_X, 0:240, 0:HALF]
+    )
     for copy in in_w:
         copy.wait()
-    got_wo()
-    got_wof = gather(wo_p, wof.at[:, piece(chip), mine], wof.at[:, 0:240, 0:HALF])
     for copy in in_k + in_q:
         copy.wait()
     got_frs()
@@ -241,7 +243,7 @@
     got_wq2()
     got_wqo2 = to_other([(wqf.at[2, hq, :], wqf.at[2, hq, :])], wqf.at[0, 0:HALF, :])
     got_wof()
-    got_woo = to_other([(wof.at[:, :, mine], wof.at[:, :, mine])], wof.at[:, :, 0:HALF])
+    got_woo = to_other([(wof.at[1:N_X, :, mine], wof.at[1:N_X, :, mine])], wof.at[1:N_X, :, 0:HALF])
     pass_on(3)
     got_kvo[1]()
     forward(1)
@@ -253,17 +255,17 @@
     q[2] = dot(frows[...], wqf[2]).astype(BF)
     got_kvo[2]()
     forward(2)
-    got_woo()
-
-    @pl.loop(0, N_X)
-    def _(n):
-        at = block(beyond(n), WIDTH)
-        heads = jnp.concatenate([att[o] for o in range(N_X)], axis=1)
-        weights = jnp.concatenate([wof[o, :, at] for o in range(N_X)], axis=0)
-        mix_s[n] = dot(heads, weights).astype(BF)
-
-    got_mix = to_x(lambda dx: mix_s.at[dx], lambda o: mix_r.at[my_rows, :], mix_r.at[0 : 3 * rows, :])
-    own_mix = load(mix_s.at[0], mix_r.at[my_rows, :])
+
+    def mix():
+        @pl.loop(0, N_X)
+        def _(n):
+            at = block(beyond(n), WIDTH)
+            heads = jnp.concatenate([att[o] for o in range(N_X)], axis=1)
+            weights = jnp.concatenate([wof[o, :, at] for o in range(N_X)], axis=0)
+            mix_s[n] = dot(heads, weights).astype(BF)
+
+        arrived = to_x(lambda dx: mix_s.at[dx], lambda o: mix_r.at[my_rows, :], mix_r.at[0 : 3 * rows, :])
+        return arrived, load(mix_s.at[0], mix_r.at[my_rows, :])
 
     for copy in in_c:
         copy.wait()
@@ -284,6 +286,8 @@
     for o in range(N_X):
         w_s[0, o] = dot(att_t[o], cot[...]).astype(BF)
         to_pair(0, o)
+
+    got_woo()
 
     @pl.loop(0, N_X)
     def _(g):
@@ -359,6 +363,8 @@
         got_gpair[o] = to_other([(gkv.at[1 - core, o], gkv_pair.at[o])], gkv_pair.at[o])
         w_s[1, o] = dot(gq_t[o], frows[...]).astype(BF)
         to_pair(1, o)
+        if i == 0:
+            got_mix, own_mix = mix()
         if i > 0:
             pair_sums(order[i - 1])
         if i > 1:
@@ -399,14 +405,14 @@
     got_wx.append(stage_x(1))
     got_gf.append(send_gf((2,)))
     outs = []
+    got_w.append(stage_w(1))
+    got_gkm()
+    got_gkmo = to_other([(gkm.at[core], gkm.at[core])], gkm.at[0])
+    got_w[0]()
+    got_wo2 = [to_other([(w_ag.at[0, core], w_ag.at[0, core])], w_ag.at[0, 0])]
     own_mix.wait()
     got_mix()
     outs.append(load(mix_r, mixed_o))
-    got_w[0]()
-    got_wo2 = [to_other([(w_ag.at[0, core], w_ag.at[0, core])], w_ag.at[0, 0])]
-    got_w.append(stage_w(1))
-    got_gkm()
-    got_gkmo = to_other([(gkm.at[core], gkm.at[core])], gkm.at[0])
     got_ffo()
     got_gkmo()
 

time: 101 us -> 95.5 us (0.946); the launches traced: 101 us -> 93.7 us
  Pallas kernels: 100 us -> 92.9 us
    pallas_call x1, Pallas kernels: 95.7 us -> 88.6 us  [body(): pl.pallas_call(kernel, out_shape=(shape((span, 256), BF), shape((span, 25...]
where the time goes in v4:
time: 95.5 us; the launch traced here: 93.7 us
  Pallas kernels  92.9 us (97%)
    pallas_call x1, Pallas kernels, body(): pl.pallas_call(kernel, out_shape=(shape((span, 256), BF), shape((span, 25...  88.6 us
    pallas_call x1, Pallas kernels, body(): pl.pallas_call(finish, out_shape=(shape((span, 256), BF), shape((span, 25...  4.25 us

profile of v4, /device:TPU:1, one launch (start us, length us, event | category | flops | bytes accessed | tf_op | source)
XLA Modules:
  0.0 93.7 jit_solution(6578681800099283505)
XLA Ops:
  0.6 88.6 %shard_map.127 = (bf16[2048,256]{1,0:T(8,128)(2,1)}, bf16[2048,256]{1,0:T(8,128)(2,1)}, bf16[1024,256]{1,0:T(8,128)(2,1)}, bf16[1024,256]{1,0:T(8,128)(2,1)}, bf16[2,2,256,512]{3,2,1,0:T(8,128)(2,1)}) custom-call(bf16[2048,1024]{1,0:T(8,128)(2,1)} %frames.1, bf16[256,2048]{1,0:T(8,128)(2,1)} %len_keys.1, bf16[256,2048]{1,0:T(8,128)(2,1)} %len_values.1, ...), custom_call_target="tpu_custom_call" | custom-call | flops 14000000000 | bytes 24000000 | tf_op jit(solution)/shard_map/pallas_call | solution.py:509
  89.3 4.2 %shard_map.128 = (bf16[2048,256]{1,0:T(8,128)(2,1)}, bf16[2048,256]{1,0:T(8,128)(2,1)}, f32[1024,256]{1,0:T(8,128)}, f32[1024,256]{1,0:T(8,128)}, f32[1024,256]{1,0:T(8,128)}, /*index=5*/f32[256,1024]{1,0:T(8,128)}) custom-call(bf16[2048,256]{1,0:T(8,128)(2,1)} %get-tuple-element.11.mixed, bf16[2048,256]{1,0:T(8,128)(2,1)} %get-tuple-element.12.gframes, ...), custom_call_target="tpu_custom_call" | custom-call | flops 1000000 | bytes 11000000 | tf_op jit(solution)/shard_map/pallas_call | solution.py:523

commit v5 on v4

--- a/solution.py
+++ b/solution.py
@@ -296,25 +296,24 @@
     for o in range(N_X):
         stage_a(0, o)
 
-    def stage_b(k):
-        for o in range(N_X):
-            got_wa[k][o]()
-
-        @pl.loop(0, N_X)
-        def _(g):
-            w_s2[k, g] = add(w_sum[k, g, block(at_a, 64), :], lambda o: w_ra[k, g, o], N_X)
-
-        return to_line(
-            lambda p: w_s2.at[k, :, piece(p), :], lambda o: w_rb.at[k, o], w_rb.at[k, 1:N_X], at_b, step_b
+    got_wb, got_wx = ({}, {}), ({}, {})
+
+    def stage_b(k, o):
+        got_wa[k][o]()
+        w_s2[k, o] = add(w_sum[k, o, block(at_a, 64), :], lambda d: w_ra[k, o, d], N_X)
+        got_wb[k][o] = to_line(
+            lambda p: w_s2.at[k, o, piece(p), :], lambda d: w_rb.at[k, o, d], w_rb.at[k, o, 1:N_X], at_b, step_b
         )
 
-    def stage_x(k):
-        got_wb[k]()
-        w_x[k] = add(w_s2[k, :, piece(at_b), :], lambda o: w_rb[k, o], N_X)
-        return to_x(lambda dx: w_x.at[k, dx], lambda o: w_xr.at[k, o], w_xr.at[k, 1:N_X])
+    def stage_x(k, o):
+        got_wb[k][o]()
+        w_x[k, o] = add(w_s2[k, o, piece(at_b), :], lambda d: w_rb[k, o, d], N_X)
+        if o:
+            got_wx[k][o] = to_x(lambda dx: w_x.at[k, dx], lambda d: w_xr.at[k, d], w_xr.at[k, N_X - o], (o,))
 
     def stage_w(k):
-        got_wx[k]()
+        for o in (1, 2, 3):
+            got_wx[k][o]()
         w_f[k] = add(w_x[k, 0], lambda o: w_xr[k, o], N_X)
         return gather(w_f.at[k], w_ag.at[k, core, piece(4 * at_a + at_b), :], w_ag.at[k, 0, 0:240, :])
 
@@ -370,10 +369,17 @@
         if i > 1:
             chip_sums(order[i - 2])
         if i == 2:
-            got_wb = [stage_b(0)]
+            for g in range(N_X):
+                stage_b(0, g)
+        if i > 1:
+            stage_b(1, order[i - 2])
     pair_sums(order[3])
     chip_sums(order[2])
-    got_wx = [stage_x(0)]
+    for g in range(N_X):
+        stage_x(0, g)
+    stage_b(1, order[2])
+    for o in order[:2]:
+        stage_x(1, o)
 
     @pl.loop(0, N_X)
     def _(n):
@@ -398,13 +404,14 @@
         m_s[o] = dot_nt(gk16[0], wkv[core, block(beyond(o), WIDTH), :]).astype(BF)
     got_m = to_x(lambda dx: m_s.at[dx], lambda o: m_r.at[o], m_r.at[1:N_X])
     got_w = [stage_w(0)]
-    got_wb.append(stage_b(1))
+    stage_b(1, 0)
+    stage_x(1, order[2])
     got_m()
     gk16[1] = add(m_s[0], lambda o: m_r[o], N_X)
     got_gkm = gather(gk16, gkm.at[core, :, piece(chip), :], gkm.at[0, :, 0:240, :])
-    got_wx.append(stage_x(1))
     got_gf.append(send_gf((2,)))
     outs = []
+    stage_x(1, 0)
     got_w.append(stage_w(1))
     got_gkm()
     got_gkmo = to_other([(gkm.at[core], gkm.at[core])], gkm.at[0])
@@ -502,7 +509,7 @@
         bf(2, 4, 256, 1024), bf(2, 4, 256, 512), bf(2, 4, 256, 512), bf(2, 4, 4, 64, 512),
         bf(2, 4, 64, 512), bf(2, 4, 4, 16, 512), bf(2, 4, 16, 512), bf(2, 4, 16, 512),
         bf(2, 16, 512), bf(2, 2, 256, 512), bf(depth, 256), bf(depth, 256),
-        pltpu.SemaphoreType.DMA((180,)),
+        pltpu.SemaphoreType.DMA((220,)),
     ]
     any_ = pl.BlockSpec(memory_space=pl.ANY)
     shape = jax.ShapeDtypeStruct

time: 95.5 us -> 96.2 us (level); the launches traced: 93.7 us -> 96.1 us
  Pallas kernels: 92.9 us -> 95.3 us
    pallas_call x1, Pallas kernels: 88.6 us -> 91 us  [body(): pl.pallas_call(kernel, out_shape=(shape((span, 256), BF), shape((span, 25...]
where the time goes in v5:
time: 96.2 us; the launch traced here: 96.1 us
  Pallas kernels  95.3 us (99%)
    pallas_call x1, Pallas kernels, body(): pl.pallas_call(kernel, out_shape=(shape((span, 256), BF), shape((span, 25...  91 us
    pallas_call x1, Pallas kernels, body(): pl.pallas_call(finish, out_shape=(shape((span, 256), BF), shape((span, 25...  4.25 us

profile of v5, /device:TPU:1, one launch (start us, length us, event | category | flops | bytes accessed | tf_op | source)
XLA Modules:
  0.0 96.1 jit_solution(3228516238531446880)
XLA Ops:
  0.6 91.0 %shard_map.127 = (bf16[2048,256]{1,0:T(8,128)(2,1)}, bf16[2048,256]{1,0:T(8,128)(2,1)}, bf16[1024,256]{1,0:T(8,128)(2,1)}, bf16[1024,256]{1,0:T(8,128)(2,1)}, bf16[2,2,256,512]{3,2,1,0:T(8,128)(2,1)}) custom-call(bf16[2048,1024]{1,0:T(8,128)(2,1)} %frames.1, bf16[256,2048]{1,0:T(8,128)(2,1)} %len_keys.1, bf16[256,2048]{1,0:T(8,128)(2,1)} %len_values.1, ...), custom_call_target="tpu_custom_call" | custom-call | flops 14000000000 | bytes 24000000 | tf_op jit(solution)/shard_map/pallas_call | solution.py:516
  91.7 4.2 %shard_map.128 = (bf16[2048,256]{1,0:T(8,128)(2,1)}, bf16[2048,256]{1,0:T(8,128)(2,1)}, f32[1024,256]{1,0:T(8,128)}, f32[1024,256]{1,0:T(8,128)}, f32[1024,256]{1,0:T(8,128)}, /*index=5*/f32[256,1024]{1,0:T(8,128)}) custom-call(bf16[2048,256]{1,0:T(8,128)(2,1)} %get-tuple-element.11.mixed, bf16[2048,256]{1,0:T(8,128)(2,1)} %get-tuple-element.12.gframes, ...), custom_call_target="tpu_custom_call" | custom-call | flops 1000000 | bytes 11000000 | tf_op jit(solution)/shard_map/pallas_call | solution.py:530

commit v6 on v4

--- a/solution.py
+++ b/solution.py
@@ -390,6 +390,8 @@
     got_gf = [send_gf((1, 3))]
     own_gf = load(gf_s.at[0], gf_r.at[my_rows, :])
 
+    early = len(sent) - 2
+
     chip_sums(0)
     for o in (1, 2, 3):
         got_gx[o]()
@@ -397,15 +399,18 @@
     for o in range(N_X):
         m_s[o] = dot_nt(gk16[0], wkv[core, block(beyond(o), WIDTH), :]).astype(BF)
     got_m = to_x(lambda dx: m_s.at[dx], lambda o: m_r.at[o], m_r.at[1:N_X])
-    got_w = [stage_w(0)]
     got_wb.append(stage_b(1))
     got_m()
     gk16[1] = add(m_s[0], lambda o: m_r[o], N_X)
     got_gkm = gather(gk16, gkm.at[core, :, piece(chip), :], gkm.at[0, :, 0:240, :])
+    got_w = [stage_w(0)]
     got_wx.append(stage_x(1))
     got_gf.append(send_gf((2,)))
     outs = []
     got_w.append(stage_w(1))
+    for ref, sem in sent[:early]:
+        landed(ref, sem)
+    del sent[:early]
     got_gkm()
     got_gkmo = to_other([(gkm.at[core], gkm.at[core])], gkm.at[0])
     got_w[0]()

time: 95.5 us -> 96.5 us (1.010); the launches traced: 93.7 us -> 96.4 us
  Pallas kernels: 92.9 us -> 95.6 us
    pallas_call x1, Pallas kernels: 88.6 us -> 91.3 us  [body(): pl.pallas_call(kernel, out_shape=(shape((span, 256), BF), shape((span, 25...]
where the time goes in v6:
time: 96.5 us; the launch traced here: 96.4 us
  Pallas kernels  95.6 us (99%)
    pallas_call x1, Pallas kernels, body(): pl.pallas_call(kernel, out_shape=(shape((span, 256), BF), shape((span, 25...  91.3 us
    pallas_call x1, Pallas kernels, body(): pl.pallas_call(finish, out_shape=(shape((span, 256), BF), shape((span, 25...  4.25 us

profile of v6, /device:TPU:1, one launch (start us, length us, event | category | flops | bytes accessed | tf_op | source)
XLA Modules:
  0.0 96.4 jit_solution(10254784714921431475)
XLA Ops:
  0.6 91.3 %shard_map.127 = (bf16[2048,256]{1,0:T(8,128)(2,1)}, bf16[2048,256]{1,0:T(8,128)(2,1)}, bf16[1024,256]{1,0:T(8,128)(2,1)}, bf16[1024,256]{1,0:T(8,128)(2,1)}, bf16[2,2,256,512]{3,2,1,0:T(8,128)(2,1)}) custom-call(bf16[2048,1024]{1,0:T(8,128)(2,1)} %frames.1, bf16[256,2048]{1,0:T(8,128)(2,1)} %len_keys.1, bf16[256,2048]{1,0:T(8,128)(2,1)} %len_values.1, ...), custom_call_target="tpu_custom_call" | custom-call | flops 14000000000 | bytes 24000000 | tf_op jit(solution)/shard_map/pallas_call | solution.py:514
  92.0 4.2 %shard_map.128 = (bf16[2048,256]{1,0:T(8,128)(2,1)}, bf16[2048,256]{1,0:T(8,128)(2,1)}, f32[1024,256]{1,0:T(8,128)}, f32[1024,256]{1,0:T(8,128)}, f32[1024,256]{1,0:T(8,128)}, /*index=5*/f32[256,1024]{1,0:T(8,128)}) custom-call(bf16[2048,256]{1,0:T(8,128)(2,1)} %get-tuple-element.11.mixed, bf16[2048,256]{1,0:T(8,128)(2,1)} %get-tuple-element.12.gframes, ...), custom_call_target="tpu_custom_call" | custom-call | flops 1000000 | bytes 11000000 | tf_op jit(solution)/shard_map/pallas_call | solution.py:528
